TPU v7x, 32 devices: a whole 2x2x4 slice. The times are simulated.
32 devices in a mesh: seq: 4 (over z), wide: 8 (over y, x, core).
Axes of the slice: x: 2, y: 2, z: 4, core: 2. Of those that a mesh axis runs over, the one named last changes fastest.
Arguments:
- layer_input: bfloat16 [8192, 8192], P(('wide', 'seq')), may hold values from -6 to 6
- head_inputs: bfloat16 [8192, 8192], P(('wide', 'seq')), may hold values from -6 to 6
- output_grad: bfloat16 [8192, 8192], P(('wide', 'seq')), may hold values from -6 to 6
- step_raw: bfloat16 [8192, 128], P(('wide', 'seq'))
- state_write: bfloat16 [8192, 64], P(('wide', 'seq')), may hold values from -5 to 5
- state_read: bfloat16 [8192, 64], P(('wide', 'seq')), may hold values from -5 to 5
- decay_log: float32 [128], replicated
- step_bias: float32 [128], replicated, may hold values from -1 to 0.5
- skip_gain: float32 [128], replicated, may hold values from 0.5 to 1.5
Outputs:
- grad_x: bfloat16 [8192, 8192], P(('wide', 'seq'))
- weight_grad: float32 [8192, 256], P(('seq', 'wide'))
All inputs are finite; a program needn't handle non-finite values.
Results may differ from a plain program's by a relative error of at most 0.0029.
Values may be sent and summed in bfloat16 or wider, within the bound.
No kernel may reach another device: no remote copies, remote signals or barrier semaphores. Data moves between devices by JAX's collectives and lax.ppermute only.
A program may use at most 384 MiB of HBM per device.

v0:
```python
import functools
import math

import jax
import jax.numpy as jnp
from jax import lax
from jax.experimental import pallas as pl
from jax.experimental.pallas import tpu as pltpu
from jax.sharding import PartitionSpec as P

F32 = jnp.float32
BF16 = jnp.bfloat16
EXACT = lax.Precision.HIGHEST
VMEM_LIMIT = 64 * 1024 * 1024
TOP_POWER = 30.0
PRODUCT_BOUND = 30.0
LAYER_BOUND = 24.0
SUMMARY_HEADS = 32
CARRY_HEADS = 32
GRAD_HEADS = 32
PAIR_HEADS = 8
META = 8
SHORT = pl.CostEstimate(flops=1000, bytes_accessed=1000, transcendentals=0)


def mul(a, b):
    return lax.dot_general(a, b, (((1,), (0,)), ((), ())), preferred_element_type=F32)


def mul_nt(a, b):
    return lax.dot_general(a, b, (((1,), (1,)), ((), ())), preferred_element_type=F32)


def mul_exact(a, b, dims=((1,), (0,))):
    return lax.dot_general(a, b, (dims, ((), ())), preferred_element_type=F32, precision=EXACT)


def halves(value):
    top = value.astype(BF16)
    return top, (value - top.astype(F32)).astype(BF16)


def power_for(bound):
    power = jnp.floor(TOP_POWER - jnp.log2(jnp.maximum(bound, 1e-37)))
    return jnp.clip(power, -100.0, 100.0)


def thirds(value):
    top, rest = value.astype(BF16), value
    rest = rest - top.astype(F32)
    middle = rest.astype(BF16)
    return top, middle, (rest - middle.astype(F32)).astype(BF16)


def encode(value):
    square = value * value
    fourth = square * square
    return jnp.where(value < 0, -fourth, fourth).astype(BF16)


def decode(coded):
    coded = coded.astype(F32)
    size = jnp.maximum(jnp.abs(coded), 1e-37)
    inverse = lax.rsqrt(size)
    return coded * inverse * lax.rsqrt(size * inverse)


def head_selector(first_head, heads, lanes, head_width):
    row = lax.broadcasted_iota(jnp.int32, (heads, lanes), 0)
    lane = lax.broadcasted_iota(jnp.int32, (heads, lanes), 1)
    return jnp.where(row == first_head + lane // head_width, 1.0, 0.0).astype(BF16)


def triangle(length, keep):
    row = lax.broadcasted_iota(jnp.int32, (length, length), 0)
    col = lax.broadcasted_iota(jnp.int32, (length, length), 1)
    return jnp.where(keep(row, col), 1.0, 0.0).astype(F32)


def summary_kernel(
    head_width,
    raw_ref,
    bias_ref,
    decay_ref,
    write_ref,
    read_ref,
    x_ref,
    dy_ref,
    message_ref,
    step_ref,
    cum_ref,
    weight_f,
    weight_b,
    facts,
):
    turn = pl.program_id(0)
    heads = raw_ref.shape[1]
    rows, lanes = x_ref.shape
    state = write_ref.shape[0]

    @pl.when(turn == 0)
    def _():
        step = jax.nn.softplus(raw_ref[...].astype(F32) + bias_ref[...])
        rate = -jnp.exp(decay_ref[...])
        cum = mul_exact(triangle(rows, lambda r, c: r >= c), step * rate)
        finish = cum[rows - 1 : rows, :]
        forward = step * jnp.exp(finish - cum)
        backward = jnp.exp(cum)
        power_f = power_for(PRODUCT_BOUND * jnp.sum(forward, axis=0, keepdims=True))
        power_b = power_for(PRODUCT_BOUND * jnp.sum(backward, axis=0, keepdims=True))
        step_ref[...] = step
        cum_ref[...] = cum
        parts = thirds(jnp.maximum(finish, -1e30))
        facts[...] = jnp.concatenate(
            [part.astype(F32) for part in parts]
            + [power_f, power_b, jnp.zeros((META - 5, heads), F32)],
            axis=0,
        ).astype(BF16)
        weight_f[...] = (forward * jnp.exp2(power_f)).T
        weight_b[...] = (backward * jnp.exp2(power_b)).T

    group = lanes // head_width
    pair_lanes = 2 * head_width
    width = message_ref.shape[2]
    near = pl.ds(turn * group, group)
    pick = head_selector(turn * group, heads, lanes, head_width)
    fact = mul(facts[...], pick).astype(BF16)
    lane = lax.broadcasted_iota(jnp.int32, (state, pair_lanes), 1)
    ahead = (x_ref, write_ref[...].astype(F32), weight_f[near, :], 0)
    behind = (dy_ref, read_ref[...].astype(F32), weight_b[near, :], state)
    for pair in range(group // 2):
        span = slice(pair * pair_lanes, (pair + 1) * pair_lanes)
        owner, offset = pair * pair_lanes // width, pair * pair_lanes % width
        here = slice(offset, offset + pair_lanes)
        for tokens_ref, rows_t, weights, start in (ahead, behind):
            scaled = []
            for head in (2 * pair, 2 * pair + 1):
                scaled += halves(rows_t * weights[head : head + 1, :])
            product = mul(jnp.concatenate(scaled, axis=0), tokens_ref[:, span])
            early = product[0:state] + product[state : 2 * state]
            late = product[2 * state : 3 * state] + product[3 * state :]
            total = jnp.where(lane < head_width, early, late)
            message_ref[owner, start : start + state, here] = encode(total)
        message_ref[owner, 2 * state :, here] = fact[:, span]


def scan_kernel(message_ref, *rest):
    answer_ref, powers = rest[-2:]
    blocks, double, lanes = message_ref.shape
    state = (double - META) // 2
    top = 2.0**TOP_POWER

    def one(block, start, power_row, side, running, bound):
        facts = message_ref[block, 2 * state : double, :].astype(F32)
        decay = jnp.exp(facts[0:1] + facts[1:2] + facts[2:3])
        back = jnp.exp2(-facts[power_row : power_row + 1])
        power = power_for(bound)
        powers[side, pl.ds(block, 1), :] = power
        answer_ref[block, start : start + state, :] = encode(running * jnp.exp2(power))
        own = decode(message_ref[block, start : start + state, :]) * back
        return running * decay + own, bound * decay + top * back

    def both(block, carry):
        ahead, ahead_bound, behind, behind_bound = carry
        return one(block, 0, 3, 0, ahead, ahead_bound) + one(
            blocks - 1 - block, state, 4, 1, behind, behind_bound
        )

    zero, none = jnp.zeros((state, lanes), F32), jnp.zeros((1, lanes), F32)
    lax.fori_loop(0, blocks, both, (zero, none, zero, none), unroll=4)
    row = lax.broadcasted_iota(jnp.int32, (blocks, META, lanes), 1)
    ahead, behind = powers[0][:, None, :], powers[1][:, None, :]
    meta = jnp.where(row == 0, ahead, jnp.where(row == 1, behind, 0.0))
    answer_ref[:, 2 * state : double, :] = meta.astype(BF16)


def block_kernel(
    head_width,
    scale,
    first_head,
    waits,
    step_ref,
    cum_ref,
    write_ref,
    read_ref,
    x_ref,
    dy_ref,
    *rest,
):
    inner_ref, own_ref, within_ref, maps_ref = rest[waits : waits + 4]
    read_write, source, cum_rows, pair_sum, out_flow = rest[waits + 4 :]
    turn = pl.program_id(0)
    rows, lanes = x_ref.shape
    half = rows // 2
    heads = step_ref.shape[1]
    group = lanes // head_width

    @pl.when(turn == 0)
    def _():
        read_write[...] = scale * lax.dot_general(
            write_ref[...], read_ref[...], (((0,), (0,)), ((), ())), preferred_element_type=F32
        )
        source[...] = jnp.log(step_ref[...]) - cum_ref[...]
        cum_rows[...] = cum_ref[...].T
        pair_sum[...] = jnp.zeros_like(pair_sum)
        out_flow[...] = jnp.zeros_like(out_flow)
        own_ref[...] = jnp.zeros_like(own_ref)

    first = first_head + turn * group
    near = pltpu.roll(source[...], lax.rem(heads - first, heads), axis=1)
    near_cum = cum_rows[pl.ds(first, group), :]
    row = lax.broadcasted_iota(jnp.int32, (half, half), 0)
    col = lax.broadcasted_iota(jnp.int32, (half, half), 1)
    ahead = col >= row
    lane = lax.broadcasted_iota(jnp.int32, (half, 2 * head_width), 1)
    first_half = lane < head_width
    head_lane = lax.broadcasted_iota(jnp.int32, (half, heads), 1)
    flow_aa = read_write[0:half, 0:half]
    flow_ab = read_write[0:half, half:rows]
    flow_bb = read_write[half:rows, half:rows]
    sum_aa = jnp.zeros((half, half), F32)
    sum_ab = jnp.zeros((half, half), F32)
    sum_bb = jnp.zeros((half, half), F32)
    own_a = jnp.zeros((half, heads), F32)
    own_b = jnp.zeros((half, heads), F32)
    zero = jnp.zeros((half, 2 * head_width), BF16)
    flows = []
    for pair in range(group // 2):
        span = slice(pair * 2 * head_width, (pair + 1) * 2 * head_width)
        x_a, x_b = x_ref[0:half, span], x_ref[half:rows, span]
        dy_a, dy_b = dy_ref[0:half, span], dy_ref[half:rows, span]
        early_a, late_a = jnp.where(first_half, dy_a, zero), jnp.where(first_half, zero, dy_a)
        early_b, late_b = jnp.where(first_half, dy_b, zero), jnp.where(first_half, zero, dy_b)
        stack = jnp.concatenate([early_a, early_b, late_a, late_b], axis=0)
        stack_b = jnp.concatenate([early_b, late_b], axis=0)
        grad_a = mul_nt(x_a, stack)
        grad_b = mul_nt(x_b, stack_b)
        masks_a, masks_b = [], []
        for side in range(2):
            place = pair * 2 + side
            head = first + place
            from_a = near[0:half, place : place + 1]
            from_b = near[half:rows, place : place + 1]
            to_a = near_cum[place : place + 1, 0:half]
            to_b = near_cum[place : place + 1, half:rows]
            fade_aa = jnp.exp(jnp.where(ahead, to_a + from_a, -1e30))
            fade_ab = jnp.exp(to_b + from_a)
            fade_bb = jnp.exp(jnp.where(ahead, to_b + from_b, -1e30))
            weigh_aa = fade_aa * grad_a[:, side * rows : side * rows + half]
            weigh_ab = fade_ab * grad_a[:, side * rows + half : (side + 1) * rows]
            weigh_bb = fade_bb * grad_b[:, side * half : (side + 1) * half]
            sum_aa += weigh_aa
            sum_ab += weigh_ab
            sum_bb += weigh_bb
            masks_a += [(fade_aa * flow_aa).astype(BF16), (fade_ab * flow_ab).astype(BF16)]
            masks_b += [(fade_bb * flow_bb).astype(BF16)]
            pair_aa = weigh_aa * flow_aa
            pair_ab = weigh_ab * flow_ab
            pair_bb = weigh_bb * flow_bb
            flow_out = jnp.sum(pair_aa + pair_ab, axis=1, keepdims=True)
            own_a = jnp.where(head_lane == head, flow_out, own_a)
            flow_out = jnp.sum(pair_bb, axis=1, keepdims=True)
            own_b = jnp.where(head_lane == head, flow_out, own_b)
            flow_in = [
                jnp.sum(pair_aa, axis=0, keepdims=True),
                jnp.sum(pair_ab, axis=0, keepdims=True) + jnp.sum(pair_bb, axis=0, keepdims=True),
            ]
            flows.append(jnp.concatenate(flow_in, axis=1))
        inner_ref[0:half, span] = mul(jnp.concatenate(masks_a, axis=1), stack).astype(BF16)
        inner_ref[half:rows, span] = mul(jnp.concatenate(masks_b, axis=1), stack_b).astype(BF16)
    out_flow[pl.ds(first, group), :] = jnp.concatenate(flows, axis=0)
    pair_sum[0:half, 0:half] += sum_aa
    pair_sum[0:half, half:rows] += sum_ab
    pair_sum[half:rows, half:rows] += sum_bb
    own_ref[0:half, :] += own_a
    own_ref[half:rows, :] += own_b

    @pl.when(turn == pl.num_programs(0) - 1)
    def _():
        net = own_ref[...] - out_flow[...].T
        within_ref[...] = mul_exact(triangle(rows, lambda r, c: r > c), net)
        weighted = scale * pair_sum[...]
        maps_ref[...] = jnp.concatenate(
            [
                mul_exact(weighted, read_ref[...].astype(F32), ((1,), (1,))),
                mul_exact(weighted, write_ref[...].astype(F32), ((0,), (1,))),
            ],
            axis=1,
        )


def spread_heads(weight, first_head, picks, group):
    heads = weight.shape[1]
    near = pltpu.roll(weight, lax.rem(heads - first_head, heads), axis=1)
    top = near.astype(BF16).astype(F32)
    low = pltpu.roll(near - top, group, axis=1)
    lane = lax.broadcasted_iota(jnp.int32, near.shape, 1)
    return mul(jnp.where(lane < group, top, low).astype(BF16), picks)


def spread_picks(group, heads, lanes, head_width):
    row = lax.broadcasted_iota(jnp.int32, (heads, lanes), 0)
    lane = lax.broadcasted_iota(jnp.int32, (heads, lanes), 1)
    match = jnp.where(row < group, row, row - group) == lane // head_width
    return jnp.where(match, 1.0, 0.0).astype(BF16)


def read_answer(answer_ref, state, power_row):
    found = []
    start = power_row * state
    for piece in range(answer_ref.shape[0]):
        facts = answer_ref[piece, 2 * state :, :].astype(F32)
        back = jnp.exp2(-facts[power_row : power_row + 1])
        found.append(decode(answer_ref[piece, start : start + state, :]) * back)
    return jnp.concatenate(found, axis=1)


def carry_kernel(head_width, scale, waits, *refs):
    raw_ref, bias_ref, decay_ref, step_ref, cum_ref, write_ref, read_ref = refs[:7]
    own_ref, within_ref, map_ref, x_ref, dy_ref, answer_ref = refs[7:13]
    table_ref, sums, through, weight_e, weight_s, maps, picks = refs[13 + waits :]
    turn = pl.program_id(0)
    rows, lanes = x_ref.shape
    heads = step_ref.shape[1]
    state = write_ref.shape[0]
    group = lanes // head_width
    pair_lanes = 2 * head_width
    future, past = slice(0, heads), slice(heads, 2 * heads)
    write_sum = slice(2 * heads, 2 * heads + 2 * state)
    read_sum = slice(2 * heads + 2 * state, 2 * heads + 4 * state)

    @pl.when(turn == 0)
    def _():
        cum = cum_ref[...]
        finish = cum[rows - 1 : rows, :]
        weight_e[...] = step_ref[...] * jnp.exp(finish - cum) * scale
        weight_s[...] = jnp.exp(cum) * scale
        write, read = write_ref[...].astype(F32).T, read_ref[...].astype(F32).T
        maps[...] = jnp.concatenate([write, write, read, read], axis=1)
        picks[0:heads, :] = spread_picks(group, heads, lanes, head_width)
        picks[heads:, :] = head_selector(0, heads, lanes, head_width)
        sums[...] = jnp.zeros_like(sums)
        through[...] = jnp.zeros_like(through)

    first_here = turn * group
    pick = picks[heads:, :]
    early = lax.broadcasted_iota(jnp.int32, (state, pair_lanes), 1) < head_width
    none = jnp.zeros((state, pair_lanes), BF16)
    start = read_answer(answer_ref, state, 0)
    end = read_answer(answer_ref, state, 1)

    def products(tokens_ref, states, weight, map_columns):
        spread = spread_heads(weight[...], first_here, picks[0:heads, :], group)
        parts = halves(states)
        total, mapped = 0.0, []
        for pair in range(group // 2):
            span = slice(pair * pair_lanes, (pair + 1) * pair_lanes)
            blocks = [
                jnp.concatenate(
                    [jnp.where(early, part[:, span], none), jnp.where(early, none, part[:, span])],
                    axis=0,
                )
                for part in parts
            ]
            twice = jnp.concatenate([tokens_ref[:, span], tokens_ref[:, span]], axis=1)
            weighted = mul_nt(twice, jnp.concatenate(blocks, axis=1)) * spread[:, span]
            total += weighted
            mapped.append((weighted * map_columns).astype(BF16))
        return total, mapped

    def summed(parts):
        return mul_nt(jnp.concatenate(parts, axis=1), pick)

    def placed(value):
        return pltpu.roll(value, first_here, axis=1)

    total, mapped = products(x_ref, end, weight_e, maps[:, 0 : 2 * state])
    sums[:, write_sum] += total
    sums[:, future] += placed(summed(mapped))

    total, mapped = products(dy_ref, start, weight_s, maps[:, 2 * state : 4 * state])
    sums[:, read_sum] += total
    sums[:, past] += placed(summed(mapped))

    both = jnp.broadcast_to(jnp.sum(start * end, axis=0, keepdims=True), (8, lanes))
    top, low = halves(both)
    through[...] += placed(mul_nt(top, pick) + mul_nt(low, pick))

    @pl.when(turn == pl.num_programs(0) - 1)
    def _():
        rate = -jnp.exp(decay_ref[...])
        step = step_ref[...]
        gate = jax.nn.sigmoid(raw_ref[...].astype(F32) + bias_ref[...])
        finish = cum_ref[rows - 1 : rows, :]
        ahead = sums[:, future]
        decay_grad = (
            within_ref[...]
            + mul_exact(triangle(rows, lambda r, c: r <= c), sums[:, past])
            + mul_exact(triangle(rows, lambda r, c: r > c), ahead)
            + jnp.exp(finish) * scale * through[0:1, :]
        )
        ratio = jnp.where(step > 1e-30, gate / jnp.maximum(step, 1e-30), 1.0)
        raw_grad = (own_ref[...] + ahead) * ratio + rate * decay_grad * gate
        map_sum = sums[:, 2 * heads :]
        write_all = map_sum[:, 0:state] + map_sum[:, state : 2 * state]
        read_all = map_sum[:, 2 * state : 3 * state] + map_sum[:, 3 * state :]
        map_grad = jnp.concatenate([write_all, read_all], axis=1) + map_ref[...]
        table_ref[...] = jnp.concatenate([raw_grad.T, map_grad.T], axis=0).astype(BF16)


def grad_kernel(head_width, scale, first_head, waits, *refs):
    step_ref, cum_ref, write_ref, skip_ref, dy_ref, inner_ref, answer_ref = refs[:7]
    grad_ref, weight_e, maps, picks = refs[7 + waits :]
    turn = pl.program_id(0)
    rows, lanes = dy_ref.shape
    heads = step_ref.shape[1]
    state = write_ref.shape[0]
    group = lanes // head_width

    @pl.when(turn == 0)
    def _():
        cum = cum_ref[...]
        finish = cum[rows - 1 : rows, :]
        weight_e[...] = step_ref[...] * jnp.exp(finish - cum) * scale
        write = write_ref[...].astype(F32).T.astype(BF16)
        maps[...] = jnp.concatenate([write, write], axis=1)
        picks[...] = spread_picks(group, heads, lanes, head_width)

    first_here = first_head + turn * group
    end_parts = jnp.concatenate(halves(read_answer(answer_ref, state, 1)), axis=0)
    skip = jnp.broadcast_to(skip_ref[...], (16, heads))
    skip = spread_heads(skip, first_here, picks[...], group)[0:1]
    carried = mul(maps[...], end_parts) * spread_heads(weight_e[...], first_here, picks[...], group)
    inner = inner_ref[...].astype(F32)
    grad_ref[...] = (inner + skip * dy_ref[...].astype(F32) + carried).astype(BF16)


def deal_kernel(place_ref, layer_ref, after_ref, *out_refs):
    width = out_refs[0].shape[2]
    for turn, out_ref in enumerate(out_refs):
        start = pl.multiple_of((place_ref[0] ^ turn) * width, width)
        out_ref[0, :, :] = layer_ref[:, pl.ds(start, width)]


def product_kernel(planes, wide, place_ref, *refs):
    table_refs, layer_refs = refs[:wide], refs[wide : 2 * wide]
    out_refs = refs[-3 - planes : -3]
    table_all, layer_all, sems = refs[-3:]
    columns, rows = table_refs[0].shape
    loads = [
        pltpu.make_async_copy(ref, table_all.at[turn], sems.at[planes, turn])
        for turn, ref in enumerate(table_refs)
    ]
    for plane in range(planes):
        source = place_ref[1] ^ plane
        loads += [
            pltpu.make_async_copy(
                ref.at[source], layer_all.at[plane, pl.ds(turn * rows, rows)], sems.at[plane, turn]
            )
            for turn, ref in enumerate(layer_refs)
        ]
    for load in loads:
        load.start()
    for load in loads[:wide]:
        load.wait()
    table = jnp.concatenate([table_all[turn] for turn in range(wide)], axis=1)
    most = jnp.max(jnp.abs(table.astype(F32)), axis=0, keepdims=True)
    most = jnp.max(most, axis=1, keepdims=True)
    power = power_for(LAYER_BOUND * wide * rows * most)
    forth = jnp.exp2(power)
    for plane, out_ref in enumerate(out_refs):
        for load in loads[(plane + 1) * wide : (plane + 2) * wide]:
            load.wait()
        out_ref[0:columns, :] = encode(mul(table, layer_all[plane]) * forth)
        out_ref[columns:, :] = jnp.broadcast_to(power, out_ref[columns:, :].shape).astype(BF16)


def gather_kernel(factor, planes, *refs):
    part_refs, out_ref = refs[:planes], refs[-1]
    columns = out_ref.shape[1]
    total = jnp.zeros((columns, out_ref.shape[0]), F32)
    for part_ref in part_refs:
        power = part_ref[columns:, :].astype(F32)[0:1]
        total += decode(part_ref[0:columns, :]) * jnp.exp2(-power)
    out_ref[...] = (total * factor).T


def swap(array, axis, turn):
    if turn == 0:
        return array
    count = lax.axis_size(axis)
    return lax.ppermute(array, axis, [(one, one ^ turn) for one in range(count)])


def whole(shape):
    return pl.BlockSpec(shape, lambda i: (0,) * len(shape))


def call(kernel, steps, in_specs, out, scratch, aliases=None):
    return pl.pallas_call(
        kernel,
        grid=(steps,),
        in_specs=in_specs,
        out_specs=[spec for spec, _, _ in out],
        out_shape=[jax.ShapeDtypeStruct(dims, dtype) for _, dims, dtype in out],
        scratch_shapes=[pltpu.VMEM(dims, dtype) for dims, dtype in scratch],
        compiler_params=pltpu.CompilerParams(vmem_limit_bytes=VMEM_LIMIT),
        cost_estimate=SHORT,
        input_output_aliases=aliases or {},
    )


def body(
    layer_input,
    head_inputs,
    output_grad,
    step_raw,
    state_write,
    state_read,
    decay_log,
    step_bias,
    skip_gain,
):
    rows, channels = head_inputs.shape
    heads = step_raw.shape[1]
    head_width = channels // heads
    state = state_write.shape[1]
    model = layer_input.shape[1]
    columns = heads + 2 * state
    axes = ("wide", "seq")
    wide, planes = lax.axis_size("wide"), lax.axis_size("seq")
    blocks = wide * planes
    own_model = model // blocks
    scale = float(rows * blocks * state) ** -0.5
    owner_lanes = channels // blocks
    piece_lanes = max(owner_lanes, 128)
    pieces = channels // piece_lanes
    depth = 2 * state + META
    bias = step_bias[None, :]
    decay = decay_log[None, :]
    skip = skip_gain[None, :]
    write_t, read_t = state_write.T, state_read.T

    summary_lanes = SUMMARY_HEADS * head_width
    carry_lanes = CARRY_HEADS * head_width
    grad_lanes = GRAD_HEADS * head_width

    def tokens(width, first=0):
        return pl.BlockSpec((rows, width), lambda i: (0, first + i))

    def messages(width, first=0):
        return pl.BlockSpec((width // piece_lanes, depth, piece_lanes), lambda i: (first + i, 0, 0))

    head_spec = whole((rows, heads))
    line_spec = whole((1, heads))
    map_spec = whole((state, rows))
    head_out = (head_spec, (rows, heads), F32)

    def exchange(array):
        return lax.all_to_all(array, axes, split_axis=0, concat_axis=0, tiled=True)

    def to_owner(array):
        if owner_lanes < piece_lanes:
            split = array.reshape(pieces, depth, piece_lanes // owner_lanes, owner_lanes)
            array = jnp.moveaxis(split, 2, 1).reshape(blocks, depth, owner_lanes)
        return exchange(array)

    def from_owner(array):
        array = exchange(array)
        if owner_lanes < piece_lanes:
            split = array.reshape(pieces, piece_lanes // owner_lanes, depth, owner_lanes)
            array = jnp.moveaxis(split, 1, 2).reshape(pieces, depth, piece_lanes)
        return array

    with jax.named_scope("summaries"):
        message, step, cum = call(
            functools.partial(summary_kernel, head_width),
            channels // summary_lanes,
            [head_spec, line_spec, line_spec, map_spec, map_spec]
            + [tokens(summary_lanes), tokens(summary_lanes)],
            [
                (messages(summary_lanes), (pieces, depth, piece_lanes), BF16),
                head_out,
                head_out,
            ],
            [((heads, rows), F32), ((heads, rows), F32), ((META, heads), BF16)],
        )(step_raw, bias, decay, write_t, read_t, head_inputs, output_grad)
    place = jnp.stack([lax.axis_index("wide"), lax.axis_index("seq")]).astype(jnp.int32)
    with jax.named_scope("layer"):
        if own_model % 128:
            cut = jnp.transpose(layer_input.reshape(rows, planes, wide, own_model), (2, 1, 0, 3))
            dealt = [
                lax.dynamic_index_in_dim(cut, place[0] ^ turn, 0, False) for turn in range(wide)
            ]
        else:
            dealt = pl.pallas_call(
                deal_kernel,
                grid_spec=pltpu.PrefetchScalarGridSpec(
                    num_scalar_prefetch=1,
                    grid=(planes,),
                    in_specs=[
                        pl.BlockSpec((rows, wide * own_model), lambda i, p: (0, i)),
                        pl.BlockSpec(memory_space=pl.ANY),
                    ],
                    out_specs=[pl.BlockSpec((1, rows, own_model), lambda i, p: (i, 0, 0))] * wide,
                ),
                out_shape=[jax.ShapeDtypeStruct((planes, rows, own_model), BF16)] * wide,
                compiler_params=pltpu.CompilerParams(vmem_limit_bytes=VMEM_LIMIT),
                cost_estimate=SHORT,
            )(place, layer_input, cum)
        layer_parts = [swap(one, "wide", turn) for turn, one in enumerate(dealt)]

    anywhere = pl.BlockSpec(memory_space=pltpu.HBM)
    firsts = [turn for turn in (1, 2, 4, 3, 5) if turn < wide]
    lasts = [layer_parts[turn] for turn in range(1, wide) if turn not in firsts]
    lasts, latest = lasts[:-1], lasts[-1:]
    with jax.named_scope("own_block"):
        width = PAIR_HEADS * head_width
        inner, own, within, maps = call(
            functools.partial(block_kernel, head_width, scale, 0, 1),
            channels // width,
            [head_spec, head_spec, map_spec, map_spec, tokens(width), tokens(width), anywhere],
            [
                (tokens(width), (rows, channels), BF16),
                head_out,
                head_out,
                (whole((rows, 2 * state)), (rows, 2 * state), F32),
            ],
            [
                ((rows, rows), F32),
                ((rows, heads), F32),
                ((heads, rows), F32),
                ((rows, rows), F32),
                ((heads, rows), F32),
            ],
        )(step, cum, write_t, read_t, head_inputs, output_grad, dealt[0])
    with jax.named_scope("scan"):
        after = [own] + [layer_parts[turn] for turn in firsts]
        scan_lanes = min(owner_lanes, 128)
        scan_spec = pl.BlockSpec((blocks, depth, scan_lanes), lambda i: (0, 0, i))
        (answer,) = call(
            scan_kernel,
            owner_lanes // scan_lanes,
            [scan_spec] + [anywhere] * len(after),
            [(scan_spec, (blocks, depth, owner_lanes), BF16)],
            [((2, blocks, scan_lanes), F32)],
        )(to_owner(message), *after)
        returned = from_owner(answer)

    with jax.named_scope("carried"):
        (table,) = call(
            functools.partial(carry_kernel, head_width, scale, len(lasts)),
            channels // carry_lanes,
            [head_spec, line_spec, line_spec, head_spec, head_spec, map_spec, map_spec]
            + [head_spec, head_spec, whole((rows, 2 * state))]
            + [tokens(carry_lanes), tokens(carry_lanes), messages(carry_lanes)]
            + [anywhere] * len(lasts),
            [(whole((columns, rows)), (columns, rows), BF16)],
            [
                ((rows, 2 * heads + 4 * state), F32),
                ((8, heads), F32),
                ((rows, heads), F32),
                ((rows, heads), F32),
                ((rows, 4 * state), F32),
                ((2 * heads, carry_lanes), BF16),
            ],
        )(
            *(step_raw, bias, decay, step, cum, write_t, read_t, own, within, maps),
            *(head_inputs, output_grad, returned, *lasts),
        )

    def grad_half(half, grad):
        steps = channels // grad_lanes // 2
        first = half * steps
        in_specs = [head_spec, head_spec, map_spec, line_spec]
        in_specs += [tokens(grad_lanes, first), tokens(grad_lanes, first)]
        in_specs += [messages(grad_lanes, first)]
        in_specs += [anywhere] * len(grad)
        (grad,) = call(
            functools.partial(grad_kernel, head_width, scale, first * GRAD_HEADS, len(grad)),
            steps,
            in_specs,
            [(tokens(grad_lanes, first), (rows, channels), BF16)],
            [((rows, heads), F32), ((rows, 2 * state), BF16), ((heads, grad_lanes), BF16)],
            {len(in_specs) - 1: 0} if half else {},
        )(step, cum, write_t, skip, output_grad, inner, returned, *grad)
        return grad

    with jax.named_scope("grad_x"):
        grad_part = grad_half(0, [table] + latest)
        grad_x = grad_half(1, [grad_part])

    with jax.named_scope("projection"):
        tables = [table]
        for turn in range(1, wide):
            tables.append(swap(tables[turn - 1], "wide", 1) if turn % 2 else swap(table, "wide", turn))
        coded = (columns + META, own_model)
        products = pl.pallas_call(
            functools.partial(product_kernel, planes, wide),
            in_specs=[pl.BlockSpec(memory_space=pltpu.SMEM)] + [anywhere] * (2 * wide + 1),
            out_specs=[pl.BlockSpec(memory_space=pltpu.VMEM)] * planes,
            out_shape=[jax.ShapeDtypeStruct(coded, BF16)] * planes,
            scratch_shapes=[
                pltpu.VMEM((wide, columns, rows), BF16),
                pltpu.VMEM((planes, wide * rows, own_model), BF16),
                pltpu.SemaphoreType.DMA((planes + 1, wide)),
            ],
            compiler_params=pltpu.CompilerParams(vmem_limit_bytes=VMEM_LIMIT),
            cost_estimate=SHORT,
        )(place, *tables, *layer_parts, grad_part)
        sums = [swap(one, "seq", turn) for turn, one in enumerate(products)]
        (weight_grad,) = call(
            functools.partial(gather_kernel, 1.0 / math.sqrt(rows * blocks), planes),
            1,
            [whole(coded)] * planes + [anywhere],
            [(whole((own_model, columns)), (own_model, columns), F32)],
            [],
        )(*sums, grad_x)
    return grad_x, weight_grad


def solution(mesh):
    in_specs = (
        P(("wide", "seq"), None),
        P(("wide", "seq"), None),
        P(("wide", "seq"), None),
        P(("wide", "seq"), None),
        P(("wide", "seq"), None),
        P(("wide", "seq"), None),
        P(),
        P(),
        P(),
    )
    out_specs = (P(("wide", "seq"), None), P(("seq", "wide"), None))
    return jax.shard_map(body, mesh=mesh, in_specs=in_specs, out_specs=out_specs, check_vma=False)
```

profile of v0, /device:TPU:0, one launch (start us, length us, event | category | flops | bytes accessed | tf_op | source)
XLA Modules:
  0.0 183.4 jit_solution(17970430679542624242)
XLA Ops:
  0.6 9.8 %summaries.1 = (bf16[32,136,256]{2,1,0:T(8,128)(2,1)}, f32[256,128]{1,0:T(8,128)}, f32[256,128]{1,0:T(8,128)}) custom-call(bf16[256,128]{1,0:T(8,128)(2,1)} %refs_0_.1, f32[1,128]{1,0:T(1,128)} %bitcast.17, f32[1,128]{1,0:T(1,128)} %bitcast.19, bf16[64,256]{1,0:T(8,128)(2,1)} %bitcast.7, bf16[64,256]{1,0:T(8,128)(2,1)} %bitcast.12, ...), custom_call_target="tpu_custom_call" | custom-call | flops 1000 | bytes 1000 | tf_op jit(solution)/shard_map/summaries/pallas_call | solution.py:576
  10.4 7.4 %all-to-all-start = ((bf16[32,136,256]{2,1,0:T(8,128)(2,1)}), bf16[32,136,256]{2,1,0:T(8,128)(2,1)}, u32[]{:S(2)}, u32[]{:S(2)}) async-start(bf16[32,136,256]{2,1,0:T(8,128)(2,1)} %get-tuple-element.25), calls=%async_computation | async-start | bytes 4456448 | tf_op jit(solution)/shard_map/scan/all_to_all | solution.py:560
  17.8 0.6 pad_add_fusion.place_ref
  18.4 5.6 %layer.1 = (bf16[4,256,256]{2,1,0:T(8,128)(2,1)}, bf16[4,256,256]{2,1,0:T(8,128)(2,1)}, bf16[4,256,256]{2,1,0:T(8,128)(2,1)}, bf16[4,256,256]{2,1,0:T(8,128)(2,1...) custom-call(s32[2]{0:T(128)} %pad_add_fusion.place_ref, ...), custom_call_target="tpu_custom_call" | custom-call | flops 1000 | bytes 1000 | tf_op jit(solution)/shard_map/layer/pallas_call | solution.py:596
  24.0 0.3 collective-permute-start
  24.3 1.7 collective-permute-start.1
  26.0 1.5 collective-permute-start.2
  27.4 0.0 collective-permute-start.3
  27.4 0.6 collective-permute-start.4
  28.1 29.4 %own_block.1 = (bf16[256,8192]{1,0:T(8,128)(2,1)}, f32[256,128]{1,0:T(8,128)}, f32[256,128]{1,0:T(8,128)}, f32[256,128]{1,0:T(8,128)}) custom-call(f32[256,128]{1,0:T(8,128)} %get-tuple-element.21.step_ref.refs_3_.refs_0_, f32[256,128]{1,0:T(8,128)} %get-tuple-element.22.after_ref.cum_ref.refs_4_.refs_1_, bf16[64,256]{1,0:T(8,128)(2,1)} %bitcast.8, ...), custom_call_target="tpu_custom_call" | custom-call | flops 1000 | bytes 1000 | tf_op jit(solution)/shard_map/own_block/pallas_call | solution.py:619
  57.5 0.0 collective-permute-done.rest_1_.refs_9_
  57.5 0.0 collective-permute-done.1.rest_2_.refs_10_
  57.5 0.0 collective-permute-done.2.rest_3_.refs_12_
  57.5 8.4 %collective-permute-done.3.rest_4_.refs_11_ = bf16[4,256,256]{2,1,0:T(8,128)(2,1)} collective-permute-done((bf16[4,256,256]{2,1,0:T(8,128)(2,1)}, bf16[4,256,256]{2,1,0:T(8,128)(2,1)}, u32[]{:S(2)}, u32[]{:S(2)}) %collective-permute-start.3) | collective-permute-done | bytes 524320 | tf_op jit(solution)/shard_map/layer/ppermute | solution.py:492
  65.9 0.6 collective-permute-done.4.rest_5_.refs_13_
  66.5 1.7 all-to-all-done.message_ref
  68.3 5.5 %scan.1 = bf16[32,136,256]{2,1,0:T(8,128)(2,1)} custom-call(bf16[32,136,256]{2,1,0:T(8,128)(2,1)} %all-to-all-done.message_ref, f32[256,128]{1,0:T(8,128)} %get-tuple-element.26.rest_0_.refs_7_, bf16[4,256,256]{2,1,0:T(8,128)(2,1)} %collective-permute-done.rest_1_.refs_9_, bf16[4,256,256]{2,1,0:T(8,128)(2,1)} %collective-permute-done.1.rest_2_.refs_10_, ...), custom_call_target="tpu_custom_call" | custom-call | flops 1000 | bytes 1000 | tf_op jit(solution)/shard_map/scan/pallas_call | solution.py:641
  73.8 4.5 %all-to-all-start.1 = ((bf16[32,136,256]{2,1,0:T(8,128)(2,1)}), bf16[32,136,256]{2,1,0:T(8,128)(2,1)}, u32[]{:S(2)}, u32[]{:S(2)}) async-start(bf16[32,136,256]{2,1,0:T(8,128)(2,1)} %scan.1), calls=%async_computation.1 | async-start | bytes 4456448 | tf_op jit(solution)/shard_map/scan/all_to_all | solution.py:560
  78.3 2.5 %collective-permute-start.5 = (bf16[4,256,256]{2,1,0:T(8,128)(2,1)S(1)}, bf16[4,256,256]{2,1,0:T(8,128)(2,1)}, u32[]{:S(2)}, u32[]{:S(2)}) collective-permute-start(bf16[4,256,256]{2,1,0:T(8,128)(2,1)S(1)} %copy-done), channel_id=1, source_target_pairs={{0,6},{1,7},{2,4},{3,5},{4,2},{5,3},{6,0},{7,1},{8,14},{9,15},{10,... | collective-permute-start | bytes 1572872 | tf_op jit(solution)/shard_map/layer/ppermute | solution.py:492
  80.8 0.0 collective-permute-start.6
  80.8 36.1 %collective-permute-done.5.refs_13_.refs_14_ = bf16[4,256,256]{2,1,0:T(8,128)(2,1)} collective-permute-done((bf16[4,256,256]{2,1,0:T(8,128)(2,1)S(1)}, bf16[4,256,256]{2,1,0:T(8,128)(2,1)}, u32[]{:S(2)}, u32[]{:S(2)}) %collective-permute-start.5) | collective-permute-done | bytes 524320 | tf_op jit(solution)/shard_map/layer/ppermute | solution.py:492
  116.9 11.3 %all-to-all-done.1.refs_12_.refs_6_ = bf16[32,136,256]{2,1,0:T(8,128)(2,1)} async-done(((bf16[32,136,256]{2,1,0:T(8,128)(2,1)}), bf16[32,136,256]{2,1,0:T(8,128)(2,1)}, u32[]{:S(2)}, u32[]{:S(2)}) %all-to-all-start.1) | async-done | bytes 2228256 | tf_op jit(solution)/shard_map/scan/all_to_all | solution.py:560
  128.2 15.5 %carried.1.refs_7_.refs_0_ = bf16[256,256]{1,0:T(8,128)(2,1)} custom-call(bf16[256,128]{1,0:T(8,128)(2,1)} %refs_0_.1, f32[1,128]{1,0:T(1,128)} %bitcast.18, f32[1,128]{1,0:T(1,128)} %bitcast.20, f32[256,128]{1,0:T(8,128)} %get-tuple-element.21.step_ref.refs_3_.refs_0_, f32[256,128]{1,0:T(8,128)} %get-tuple-element.22.after_ref.cum_ref.refs_4_.refs_1_, ...), custom_call_target="tpu_custom_call" | custom-call | flops 1000 | bytes 1000 | tf_op jit(solution)/shard_map/carried/pallas_call | solution.py:651
  143.7 2.2 %collective-permute-start.12 = (bf16[256,256]{1,0:T(8,128)(2,1)}, bf16[256,256]{1,0:T(8,128)(2,1)}, u32[]{:S(2)}, u32[]{:S(2)}) collective-permute-start(bf16[256,256]{1,0:T(8,128)(2,1)} %carried.1.refs_7_.refs_0_), channel_id=1, source_target_pairs={{0,6},{1,7},{2,4},{3,5},{4,2},{5,3},{6,0},{7,1},{8,14},{9,15},{10,... | collective-permute-start | bytes 393224 | tf_op jit(solution)/shard_map/projection/ppermute | solution.py:492
  145.9 0.6 collective-permute-start.10
  146.4 0.7 collective-permute-start.8
  147.2 1.0 collective-permute-start.7
  148.2 2.7 %collective-permute-done.12.refs_6_ = bf16[256,256]{1,0:T(8,128)(2,1)} collective-permute-done((bf16[256,256]{1,0:T(8,128)(2,1)}, bf16[256,256]{1,0:T(8,128)(2,1)}, u32[]{:S(2)}, u32[]{:S(2)}) %collective-permute-start.12) | collective-permute-done | bytes 131104 | tf_op jit(solution)/shard_map/projection/ppermute | solution.py:492
  150.9 0.3 collective-permute-start.13
  151.2 2.9 %collective-permute-done.10.refs_4_ = bf16[256,256]{1,0:T(8,128)(2,1)} collective-permute-done((bf16[256,256]{1,0:T(8,128)(2,1)}, bf16[256,256]{1,0:T(8,128)(2,1)}, u32[]{:S(2)}, u32[]{:S(2)}) %collective-permute-start.10) | collective-permute-done | bytes 131104 | tf_op jit(solution)/shard_map/projection/ppermute | solution.py:492
  154.1 0.1 collective-permute-start.11
  154.2 0.2 collective-permute-done.8.refs_2_
  154.4 0.2 collective-permute-start.9
  154.6 0.0 collective-permute-done.6.refs_8_.refs_15_
  154.6 5.2 %grad_x.2.refs_7_.refs_16_ = bf16[256,8192]{1,0:T(8,128)(2,1)} custom-call(f32[256,128]{1,0:T(8,128)} %get-tuple-element.21.step_ref.refs_3_.refs_0_, f32[256,128]{1,0:T(8,128)} %get-tuple-element.22.after_ref.cum_ref.refs_4_.refs_1_, bf16[64,256]{1,0:T(8,128)(2,1)} %bitcast.10, f32[1,128]{1,0:T(1,128)} %bitcast.15, bf16[256,8192]{1,0:T(8,128)(2,1)} %refs_4_.3, ...), custom_call_target="tpu_custom_call" | custom-call | flops 1000 | bytes 1000 | tf_op jit(solution)/shard_map/grad_x/pallas_call | solution.py:679
  159.8 0.0 collective-permute-done.7.refs_1_
  159.8 0.0 collective-permute-done.13.refs_7_
  159.8 0.0 collective-permute-done.11.refs_5_
  159.8 0.0 collective-permute-done.9.refs_3_
  159.8 6.1 %projection.2 = (bf16[264,256]{1,0:T(8,128)(2,1)}, bf16[264,256]{1,0:T(8,128)(2,1)}, bf16[264,256]{1,0:T(8,128)(2,1)}, bf16[264,256]{1,0:T(8,128)(2,1)}) custom-call(s32[2]{0:T(128)} %pad_add_fusion.place_ref, bf16[256,256]{1,0:T(8,128)(2,1)} %carried.1.refs_7_.refs_0_, bf16[256,256]{1,0:T(8,128)(2,1)} %collective-permute-done.7.refs_1_, ...), custom_call_target="tpu_custom_call" | custom-call | flops 1000 | bytes 1000 | tf_op jit(solution)/shard_map/projection/pallas_call | solution.py:698
  165.9 1.7 collective-permute-start.14
  167.7 0.7 collective-permute-start.15
  168.4 2.0 %collective-permute-start.16 = (bf16[264,256]{1,0:T(8,128)(2,1)}, bf16[264,256]{1,0:T(8,128)(2,1)}, u32[]{:S(2)}, u32[]{:S(2)}) collective-permute-start(bf16[264,256]{1,0:T(8,128)(2,1)} %get-tuple-element.39), channel_id=1, source_target_pairs={{0,24},{8,16},{16,8},{24,0},{1,25},{9,17},{17,9},{25,1},{2,26},{10... | collective-permute-start | bytes 405512 | tf_op jit(solution)/shard_map/projection/ppermute | solution.py:492
  170.4 5.2 %grad_x.3.refs_4_ = bf16[256,8192]{1,0:T(8,128)(2,1)} custom-call(f32[256,128]{1,0:T(8,128)} %get-tuple-element.21.step_ref.refs_3_.refs_0_, f32[256,128]{1,0:T(8,128)} %get-tuple-element.22.after_ref.cum_ref.refs_4_.refs_1_, bf16[64,256]{1,0:T(8,128)(2,1)} %bitcast.11, f32[1,128]{1,0:T(1,128)} %bitcast.16, ...), custom_call_target="tpu_custom_call", output_to_operand_aliasing={{}: (7, {})} | custom-call | flops 1000 | bytes 1000 | tf_op jit(solution)/shard_map/grad_x/pallas_call | solution.py:679
  175.6 0.0 collective-permute-done.14.refs_1_
  175.6 5.6 %collective-permute-done.15.refs_2_ = bf16[264,256]{1,0:T(8,128)(2,1)} collective-permute-done((bf16[264,256]{1,0:T(8,128)(2,1)}, bf16[264,256]{1,0:T(8,128)(2,1)}, u32[]{:S(2)}, u32[]{:S(2)}) %collective-permute-start.15) | collective-permute-done | bytes 135200 | tf_op jit(solution)/shard_map/projection/ppermute | solution.py:492
  181.1 0.0 collective-permute-done.16.refs_3_
  181.1 2.2 %projection.3 = f32[256,256]{1,0:T(8,128)} custom-call(bf16[264,256]{1,0:T(8,128)(2,1)} %get-tuple-element.36.refs_0_, bf16[264,256]{1,0:T(8,128)(2,1)} %collective-permute-done.14.refs_1_, bf16[264,256]{1,0:T(8,128)(2,1)} %collective-permute-done.15.refs_2_, bf16[264,256]{1,0:T(8,128)(2,1)} %collective-permute-done.16.refs_3_, bf16[256,8192]{1,0:T(8,128)(2,1)} %grad_x.3.refs_4_), custom_call_target="tpu_custom_call" | custom-call | flops 1000 | bytes 1000 | tf_op jit(solution)/shard_map/projection/pallas_call | solution.py:712
  (2 shorter events, 0.0 us)
Async XLA Ops:
  10.4 57.9 %all-to-all-start = ((bf16[32,136,256]{2,1,0:T(8,128)(2,1)}), bf16[32,136,256]{2,1,0:T(8,128)(2,1)}, u32[]{:S(2)}, u32[]{:S(2)}) async-start(bf16[32,136,256]{2,1,0:T(8,128)(2,1)} %get-tuple-element.25), calls=%async_computation | async-start | bytes 4456448 | tf_op jit(solution)/shard_map/scan/all_to_all | solution.py:560
  24.0 33.5 %collective-permute-start = (bf16[4,256,256]{2,1,0:T(8,128)(2,1)}, bf16[4,256,256]{2,1,0:T(8,128)(2,1)}, u32[]{:S(2)}, u32[]{:S(2)}) collective-permute-start(bf16[4,256,256]{2,1,0:T(8,128)(2,1)} %get-tuple-element.27), channel_id=1, source_target_pairs={{0,1},{1,0},{2,3},{3,2},{4,5},{5,4},{6,7},{7,6},{8,9},{9,8},{10,11... | collective-permute-start | bytes 1572872 | tf_op jit(solution)/shard_map/layer/ppermute | solution.py:492
  24.3 33.2 %collective-permute-start.1 = (bf16[4,256,256]{2,1,0:T(8,128)(2,1)}, bf16[4,256,256]{2,1,0:T(8,128)(2,1)}, u32[]{:S(2)}, u32[]{:S(2)}) collective-permute-start(bf16[4,256,256]{2,1,0:T(8,128)(2,1)} %get-tuple-element.28), channel_id=1, source_target_pairs={{0,2},{1,3},{2,0},{3,1},{4,6},{5,7},{6,4},{7,5},{8,10},{9,11},{10,... | collective-permute-start | bytes 1572872 | tf_op jit(solution)/shard_map/layer/ppermute | solution.py:492
  26.0 31.6 %collective-permute-start.2 = (bf16[4,256,256]{2,1,0:T(8,128)(2,1)}, bf16[4,256,256]{2,1,0:T(8,128)(2,1)}, u32[]{:S(2)}, u32[]{:S(2)}) collective-permute-start(bf16[4,256,256]{2,1,0:T(8,128)(2,1)} %get-tuple-element.29), channel_id=1, source_target_pairs={{0,4},{1,5},{2,6},{3,7},{4,0},{5,1},{6,2},{7,3},{8,12},{9,13},{10,... | collective-permute-start | bytes 1572872 | tf_op jit(solution)/shard_map/layer/ppermute | solution.py:492
  27.4 38.5 %collective-permute-start.3 = (bf16[4,256,256]{2,1,0:T(8,128)(2,1)}, bf16[4,256,256]{2,1,0:T(8,128)(2,1)}, u32[]{:S(2)}, u32[]{:S(2)}) collective-permute-start(bf16[4,256,256]{2,1,0:T(8,128)(2,1)} %get-tuple-element.30), channel_id=1, source_target_pairs={{0,3},{1,2},{2,1},{3,0},{4,7},{5,6},{6,5},{7,4},{8,11},{9,10},{10,... | collective-permute-start | bytes 1572872 | tf_op jit(solution)/shard_map/layer/ppermute | solution.py:492
  27.4 39.1 %collective-permute-start.4 = (bf16[4,256,256]{2,1,0:T(8,128)(2,1)}, bf16[4,256,256]{2,1,0:T(8,128)(2,1)}, u32[]{:S(2)}, u32[]{:S(2)}) collective-permute-start(bf16[4,256,256]{2,1,0:T(8,128)(2,1)} %get-tuple-element.31), channel_id=1, source_target_pairs={{0,5},{1,4},{2,7},{3,6},{4,1},{5,0},{6,3},{7,2},{8,13},{9,12},{10,... | collective-permute-start | bytes 1572872 | tf_op jit(solution)/shard_map/layer/ppermute | solution.py:492
  73.8 4.5 %copy-start = (bf16[4,256,256]{2,1,0:T(8,128)(2,1)S(1)}, bf16[4,256,256]{2,1,0:T(8,128)(2,1)}, u32[]{:S(2)}) copy-start(bf16[4,256,256]{2,1,0:T(8,128)(2,1)} %get-tuple-element.34) | copy-start | bytes 1572868
  73.8 54.4 %all-to-all-start.1 = ((bf16[32,136,256]{2,1,0:T(8,128)(2,1)}), bf16[32,136,256]{2,1,0:T(8,128)(2,1)}, u32[]{:S(2)}, u32[]{:S(2)}) async-start(bf16[32,136,256]{2,1,0:T(8,128)(2,1)} %scan.1), calls=%async_computation.1 | async-start | bytes 4456448 | tf_op jit(solution)/shard_map/scan/all_to_all | solution.py:560
  78.3 38.6 %collective-permute-start.5 = (bf16[4,256,256]{2,1,0:T(8,128)(2,1)S(1)}, bf16[4,256,256]{2,1,0:T(8,128)(2,1)}, u32[]{:S(2)}, u32[]{:S(2)}) collective-permute-start(bf16[4,256,256]{2,1,0:T(8,128)(2,1)S(1)} %copy-done), channel_id=1, source_target_pairs={{0,6},{1,7},{2,4},{3,5},{4,2},{5,3},{6,0},{7,1},{8,14},{9,15},{10,... | collective-permute-start | bytes 1572872 | tf_op jit(solution)/shard_map/layer/ppermute | solution.py:492
  80.8 73.8 %collective-permute-start.6 = (bf16[4,256,256]{2,1,0:T(8,128)(2,1)}, bf16[4,256,256]{2,1,0:T(8,128)(2,1)}, u32[]{:S(2)}, u32[]{:S(2)}) collective-permute-start(bf16[4,256,256]{2,1,0:T(8,128)(2,1)} %get-tuple-element.35), channel_id=1, source_target_pairs={{0,7},{1,6},{2,5},{3,4},{4,3},{5,2},{6,1},{7,0},{8,15},{9,14},{10,... | collective-permute-start | bytes 1572872 | tf_op jit(solution)/shard_map/layer/ppermute | solution.py:492
  143.7 7.2 %collective-permute-start.12 = (bf16[256,256]{1,0:T(8,128)(2,1)}, bf16[256,256]{1,0:T(8,128)(2,1)}, u32[]{:S(2)}, u32[]{:S(2)}) collective-permute-start(bf16[256,256]{1,0:T(8,128)(2,1)} %carried.1.refs_7_.refs_0_), channel_id=1, source_target_pairs={{0,6},{1,7},{2,4},{3,5},{4,2},{5,3},{6,0},{7,1},{8,14},{9,15},{10,... | collective-permute-start | bytes 393224 | tf_op jit(solution)/shard_map/projection/ppermute | solution.py:492
  145.9 8.2 %collective-permute-start.10 = (bf16[256,256]{1,0:T(8,128)(2,1)}, bf16[256,256]{1,0:T(8,128)(2,1)}, u32[]{:S(2)}, u32[]{:S(2)}) collective-permute-start(bf16[256,256]{1,0:T(8,128)(2,1)} %carried.1.refs_7_.refs_0_), channel_id=1, source_target_pairs={{0,4},{1,5},{2,6},{3,7},{4,0},{5,1},{6,2},{7,3},{8,12},{9,13},{10,... | collective-permute-start | bytes 393224 | tf_op jit(solution)/shard_map/projection/ppermute | solution.py:492
  146.4 8.0 %collective-permute-start.8 = (bf16[256,256]{1,0:T(8,128)(2,1)}, bf16[256,256]{1,0:T(8,128)(2,1)}, u32[]{:S(2)}, u32[]{:S(2)}) collective-permute-start(bf16[256,256]{1,0:T(8,128)(2,1)} %carried.1.refs_7_.refs_0_), channel_id=1, source_target_pairs={{0,2},{1,3},{2,0},{3,1},{4,6},{5,7},{6,4},{7,5},{8,10},{9,11},{10,... | collective-permute-start | bytes 393224 | tf_op jit(solution)/shard_map/projection/ppermute | solution.py:492
  147.2 12.6 %collective-permute-start.7 = (bf16[256,256]{1,0:T(8,128)(2,1)}, bf16[256,256]{1,0:T(8,128)(2,1)}, u32[]{:S(2)}, u32[]{:S(2)}) collective-permute-start(bf16[256,256]{1,0:T(8,128)(2,1)} %carried.1.refs_7_.refs_0_), channel_id=1, source_target_pairs={{0,1},{1,0},{2,3},{3,2},{4,5},{5,4},{6,7},{7,6},{8,9},{9,8},{10,11... | collective-permute-start | bytes 393224 | tf_op jit(solution)/shard_map/projection/ppermute | solution.py:492
  150.9 8.9 %collective-permute-start.13 = (bf16[256,256]{1,0:T(8,128)(2,1)}, bf16[256,256]{1,0:T(8,128)(2,1)}, u32[]{:S(2)}, u32[]{:S(2)}) collective-permute-start(bf16[256,256]{1,0:T(8,128)(2,1)} %collective-permute-done.12.refs_6_), channel_id=1, source_target_pairs={{0,1},{1,0},{2,3},{3,2},{4,5},{5,4},{6,7},{7,6},{8,9},{9,8},{10,11... | collective-permute-start | bytes 393224 | tf_op jit(solution)/shard_map/projection/ppermute | solution.py:492
  154.1 5.7 %collective-permute-start.11 = (bf16[256,256]{1,0:T(8,128)(2,1)}, bf16[256,256]{1,0:T(8,128)(2,1)}, u32[]{:S(2)}, u32[]{:S(2)}) collective-permute-start(bf16[256,256]{1,0:T(8,128)(2,1)} %collective-permute-done.10.refs_4_), channel_id=1, source_target_pairs={{0,1},{1,0},{2,3},{3,2},{4,5},{5,4},{6,7},{7,6},{8,9},{9,8},{10,11... | collective-permute-start | bytes 393224 | tf_op jit(solution)/shard_map/projection/ppermute | solution.py:492
  154.4 5.4 %collective-permute-start.9 = (bf16[256,256]{1,0:T(8,128)(2,1)}, bf16[256,256]{1,0:T(8,128)(2,1)}, u32[]{:S(2)}, u32[]{:S(2)}) collective-permute-start(bf16[256,256]{1,0:T(8,128)(2,1)} %collective-permute-done.8.refs_2_), channel_id=1, source_target_pairs={{0,1},{1,0},{2,3},{3,2},{4,5},{5,4},{6,7},{7,6},{8,9},{9,8},{10,11... | collective-permute-start | bytes 393224 | tf_op jit(solution)/shard_map/projection/ppermute | solution.py:492
  165.9 9.6 %collective-permute-start.14 = (bf16[264,256]{1,0:T(8,128)(2,1)}, bf16[264,256]{1,0:T(8,128)(2,1)}, u32[]{:S(2)}, u32[]{:S(2)}) collective-permute-start(bf16[264,256]{1,0:T(8,128)(2,1)} %get-tuple-element.37), channel_id=1, source_target_pairs={{0,8},{8,0},{16,24},{24,16},{1,9},{9,1},{17,25},{25,17},{2,10},{10... | collective-permute-start | bytes 405512 | tf_op jit(solution)/shard_map/projection/ppermute | solution.py:492
  167.7 13.5 %collective-permute-start.15 = (bf16[264,256]{1,0:T(8,128)(2,1)}, bf16[264,256]{1,0:T(8,128)(2,1)}, u32[]{:S(2)}, u32[]{:S(2)}) collective-permute-start(bf16[264,256]{1,0:T(8,128)(2,1)} %get-tuple-element.38), channel_id=1, source_target_pairs={{0,16},{8,24},{16,0},{24,8},{1,17},{9,25},{17,1},{25,9},{2,18},{10... | collective-permute-start | bytes 405512 | tf_op jit(solution)/shard_map/projection/ppermute | solution.py:492
  168.4 12.7 %collective-permute-start.16 = (bf16[264,256]{1,0:T(8,128)(2,1)}, bf16[264,256]{1,0:T(8,128)(2,1)}, u32[]{:S(2)}, u32[]{:S(2)}) collective-permute-start(bf16[264,256]{1,0:T(8,128)(2,1)} %get-tuple-element.39), channel_id=1, source_target_pairs={{0,24},{8,16},{16,8},{24,0},{1,25},{9,17},{17,9},{25,1},{2,26},{10... | collective-permute-start | bytes 405512 | tf_op jit(solution)/shard_map/projection/ppermute | solution.py:492
where the time goes:
time: 184 us; the launch traced here: 183 us
  Pallas kernels  84.6 us (46%)
  waiting for transfers between devices  69.5 us (38%)
  starting transfers between devices  28 us (15%)
    ppermute x17, waiting for transfers between devices, swap(): lax.ppermute(array, axis, [(one, one ^ turn) for one in range(count)])  56.5 us
    pallas_call x1, Pallas kernels, body(): call(functools.partial(block_kernel, head_width, scale, 0, 1), channels /...  29.4 us
    ppermute x17, starting transfers between devices, swap(): lax.ppermute(array, axis, [(one, one ^ turn) for one in range(count)])  16 us
    pallas_call x1, Pallas kernels, body(): call(functools.partial(carry_kernel, head_width, scale, len(lasts)), chan...  15.5 us
    all_to_all x2, waiting for transfers between devices, exchange(): return lax.all_to_all(array, axes, split_axis=0, concat_axis=0, tiled=True)  13 us
    all_to_all x2, starting transfers between devices, exchange(): return lax.all_to_all(array, axes, split_axis=0, concat_axis=0, tiled=True)  11.9 us
    pallas_call x2, Pallas kernels, grad_half(): call(functools.partial(grad_kernel, head_width, scale, first * GRAD_HEADS...  10.4 us
    pallas_call x1, Pallas kernels, body(): call(functools.partial(summary_kernel, head_width), channels // summary_l...  9.79 us
  transfers between devices with their start and end apart: 19, of which 9 were waited for; matrix products, arithmetic and copies ran while one was open for 0% of the time, Pallas kernels for 33%

commit v1 on v0

--- a/solution.py
+++ b/solution.py
@@ -167,7 +167,7 @@
         )
 
     zero, none = jnp.zeros((state, lanes), F32), jnp.zeros((1, lanes), F32)
-    lax.fori_loop(0, blocks, both, (zero, none, zero, none), unroll=4)
+    lax.fori_loop(0, blocks, both, (zero, none, zero, none), unroll=8)
     row = lax.broadcasted_iota(jnp.int32, (blocks, META, lanes), 1)
     ahead, behind = powers[0][:, None, :], powers[1][:, None, :]
     meta = jnp.where(row == 0, ahead, jnp.where(row == 1, behind, 0.0))
@@ -669,26 +669,24 @@
             *(head_inputs, output_grad, returned, *lasts),
         )
 
-    def grad_half(half, grad):
-        steps = channels // grad_lanes // 2
-        first = half * steps
+    def grad_part_of(first, last, grad, keep):
         in_specs = [head_spec, head_spec, map_spec, line_spec]
         in_specs += [tokens(grad_lanes, first), tokens(grad_lanes, first)]
         in_specs += [messages(grad_lanes, first)]
         in_specs += [anywhere] * len(grad)
         (grad,) = call(
             functools.partial(grad_kernel, head_width, scale, first * GRAD_HEADS, len(grad)),
-            steps,
+            last - first,
             in_specs,
             [(tokens(grad_lanes, first), (rows, channels), BF16)],
             [((rows, heads), F32), ((rows, 2 * state), BF16), ((heads, grad_lanes), BF16)],
-            {len(in_specs) - 1: 0} if half else {},
+            {len(in_specs) - 1: 0} if keep else {},
         )(step, cum, write_t, skip, output_grad, inner, returned, *grad)
         return grad
 
+    grad_steps = channels // grad_lanes
     with jax.named_scope("grad_x"):
-        grad_part = grad_half(0, [table] + latest)
-        grad_x = grad_half(1, [grad_part])
+        grad_first = grad_part_of(0, 1, [table] + latest, False)
 
     with jax.named_scope("projection"):
         tables = [table]
@@ -707,7 +705,8 @@
             ],
             compiler_params=pltpu.CompilerParams(vmem_limit_bytes=VMEM_LIMIT),
             cost_estimate=SHORT,
-        )(place, *tables, *layer_parts, grad_part)
+        )(place, *tables, *layer_parts, grad_first)
+        grad_x = grad_part_of(1, grad_steps, [products[0], grad_first], True)
         sums = [swap(one, "seq", turn) for turn, one in enumerate(products)]
         (weight_grad,) = call(
             functools.partial(gather_kernel, 1.0 / math.sqrt(rows * blocks), planes),

time: 184 us -> 183 us (level)
  waiting for transfers between devices: 69.5 us -> 67.1 us
    ppermute x17, waiting for transfers between devices: 56.5 us -> 54.1 us  [swap(): lax.ppermute(array, axis, [(one, one ^ turn) for one in range(count)])]
  transfers between devices with their start and end apart: 19 -> 19, of which waited for: 9 -> 9; matrix products, arithmetic and copies ran while one was open for 0% -> 0% of each run, Pallas kernels for 33% -> 34%
where the time goes in v1:
time: 183 us; the launch traced here: 182 us
  Pallas kernels  85.5 us (47%)
  waiting for transfers between devices  67.1 us (37%)
  starting transfers between devices  28 us (15%)
    ppermute x17, waiting for transfers between devices, swap(): lax.ppermute(array, axis, [(one, one ^ turn) for one in range(count)])  54.1 us
    pallas_call x1, Pallas kernels, body(): call(functools.partial(block_kernel, head_width, scale, 0, 1), channels /...  29.4 us
    ppermute x17, starting transfers between devices, swap(): lax.ppermute(array, axis, [(one, one ^ turn) for one in range(count)])  16.1 us
    pallas_call x1, Pallas kernels, body(): call(functools.partial(carry_kernel, head_width, scale, len(lasts)), chan...  15.5 us
    all_to_all x2, waiting for transfers between devices, exchange(): return lax.all_to_all(array, axes, split_axis=0, concat_axis=0, tiled=True)  13 us
    all_to_all x2, starting transfers between devices, exchange(): return lax.all_to_all(array, axes, split_axis=0, concat_axis=0, tiled=True)  11.9 us
    pallas_call x2, Pallas kernels, grad_part_of(): call(functools.partial(grad_kernel, head_width, scale, first * GRAD_HEADS...  11.4 us
    pallas_call x1, Pallas kernels, body(): call(functools.partial(summary_kernel, head_width), channels // summary_l...  9.79 us
  transfers between devices with their start and end apart: 19, of which 9 were waited for; matrix products, arithmetic and copies ran while one was open for 0% of the time, Pallas kernels for 34%

profile of v1, /device:TPU:0, one launch (start us, length us, event | category | flops | bytes accessed | tf_op | source)
XLA Modules:
  0.0 182.0 jit_solution(5375556811204042099)
XLA Ops:
  0.6 9.8 %summaries.1 = (bf16[32,136,256]{2,1,0:T(8,128)(2,1)}, f32[256,128]{1,0:T(8,128)}, f32[256,128]{1,0:T(8,128)}) custom-call(bf16[256,128]{1,0:T(8,128)(2,1)} %refs_0_.1, f32[1,128]{1,0:T(1,128)} %bitcast.17, f32[1,128]{1,0:T(1,128)} %bitcast.19, bf16[64,256]{1,0:T(8,128)(2,1)} %bitcast.7, bf16[64,256]{1,0:T(8,128)(2,1)} %bitcast.12, ...), custom_call_target="tpu_custom_call" | custom-call | flops 1000 | bytes 1000 | tf_op jit(solution)/shard_map/summaries/pallas_call | solution.py:576
  10.4 7.4 %all-to-all-start = ((bf16[32,136,256]{2,1,0:T(8,128)(2,1)}), bf16[32,136,256]{2,1,0:T(8,128)(2,1)}, u32[]{:S(2)}, u32[]{:S(2)}) async-start(bf16[32,136,256]{2,1,0:T(8,128)(2,1)} %get-tuple-element.25), calls=%async_computation | async-start | bytes 4456448 | tf_op jit(solution)/shard_map/scan/all_to_all | solution.py:560
  17.8 0.6 pad_add_fusion.place_ref
  18.4 5.6 %layer.1 = (bf16[4,256,256]{2,1,0:T(8,128)(2,1)}, bf16[4,256,256]{2,1,0:T(8,128)(2,1)}, bf16[4,256,256]{2,1,0:T(8,128)(2,1)}, bf16[4,256,256]{2,1,0:T(8,128)(2,1...) custom-call(s32[2]{0:T(128)} %pad_add_fusion.place_ref, ...), custom_call_target="tpu_custom_call" | custom-call | flops 1000 | bytes 1000 | tf_op jit(solution)/shard_map/layer/pallas_call | solution.py:596
  24.0 0.3 collective-permute-start
  24.3 1.7 collective-permute-start.1
  26.0 1.5 collective-permute-start.2
  27.4 0.0 collective-permute-start.3
  27.4 0.6 collective-permute-start.4
  28.1 29.4 %own_block.1 = (bf16[256,8192]{1,0:T(8,128)(2,1)}, f32[256,128]{1,0:T(8,128)}, f32[256,128]{1,0:T(8,128)}, f32[256,128]{1,0:T(8,128)}) custom-call(f32[256,128]{1,0:T(8,128)} %get-tuple-element.21.step_ref.refs_3_.refs_0_, f32[256,128]{1,0:T(8,128)} %get-tuple-element.22.after_ref.cum_ref.refs_4_.refs_1_, bf16[64,256]{1,0:T(8,128)(2,1)} %bitcast.8, ...), custom_call_target="tpu_custom_call" | custom-call | flops 1000 | bytes 1000 | tf_op jit(solution)/shard_map/own_block/pallas_call | solution.py:619
  57.5 0.0 collective-permute-done.rest_1_.refs_9_
  57.5 0.0 collective-permute-done.1.rest_2_.refs_10_
  57.5 0.0 collective-permute-done.2.rest_3_.refs_12_
  57.5 8.4 %collective-permute-done.3.rest_4_.refs_11_ = bf16[4,256,256]{2,1,0:T(8,128)(2,1)} collective-permute-done((bf16[4,256,256]{2,1,0:T(8,128)(2,1)}, bf16[4,256,256]{2,1,0:T(8,128)(2,1)}, u32[]{:S(2)}, u32[]{:S(2)}) %collective-permute-start.3) | collective-permute-done | bytes 524320 | tf_op jit(solution)/shard_map/layer/ppermute | solution.py:492
  65.9 0.6 collective-permute-done.4.rest_5_.refs_13_
  66.5 1.7 all-to-all-done.message_ref
  68.3 5.4 %scan.1 = bf16[32,136,256]{2,1,0:T(8,128)(2,1)} custom-call(bf16[32,136,256]{2,1,0:T(8,128)(2,1)} %all-to-all-done.message_ref, f32[256,128]{1,0:T(8,128)} %get-tuple-element.26.rest_0_.refs_7_, bf16[4,256,256]{2,1,0:T(8,128)(2,1)} %collective-permute-done.rest_1_.refs_9_, bf16[4,256,256]{2,1,0:T(8,128)(2,1)} %collective-permute-done.1.rest_2_.refs_10_, ...), custom_call_target="tpu_custom_call" | custom-call | flops 1000 | bytes 1000 | tf_op jit(solution)/shard_map/scan/pallas_call | solution.py:641
  73.7 4.5 %all-to-all-start.1 = ((bf16[32,136,256]{2,1,0:T(8,128)(2,1)}), bf16[32,136,256]{2,1,0:T(8,128)(2,1)}, u32[]{:S(2)}, u32[]{:S(2)}) async-start(bf16[32,136,256]{2,1,0:T(8,128)(2,1)} %scan.1), calls=%async_computation.1 | async-start | bytes 4456448 | tf_op jit(solution)/shard_map/scan/all_to_all | solution.py:560
  78.3 2.5 %collective-permute-start.5 = (bf16[4,256,256]{2,1,0:T(8,128)(2,1)S(1)}, bf16[4,256,256]{2,1,0:T(8,128)(2,1)}, u32[]{:S(2)}, u32[]{:S(2)}) collective-permute-start(bf16[4,256,256]{2,1,0:T(8,128)(2,1)S(1)} %copy-done), channel_id=1, source_target_pairs={{0,6},{1,7},{2,4},{3,5},{4,2},{5,3},{6,0},{7,1},{8,14},{9,15},{10,... | collective-permute-start | bytes 1572872 | tf_op jit(solution)/shard_map/layer/ppermute | solution.py:492
  80.8 0.0 collective-permute-start.13
  80.8 36.1 %collective-permute-done.5.refs_13_.refs_14_ = bf16[4,256,256]{2,1,0:T(8,128)(2,1)} collective-permute-done((bf16[4,256,256]{2,1,0:T(8,128)(2,1)S(1)}, bf16[4,256,256]{2,1,0:T(8,128)(2,1)}, u32[]{:S(2)}, u32[]{:S(2)}) %collective-permute-start.5) | collective-permute-done | bytes 524320 | tf_op jit(solution)/shard_map/layer/ppermute | solution.py:492
  116.9 11.3 %all-to-all-done.1.refs_12_.refs_6_ = bf16[32,136,256]{2,1,0:T(8,128)(2,1)} async-done(((bf16[32,136,256]{2,1,0:T(8,128)(2,1)}), bf16[32,136,256]{2,1,0:T(8,128)(2,1)}, u32[]{:S(2)}, u32[]{:S(2)}) %all-to-all-start.1) | async-done | bytes 2228256 | tf_op jit(solution)/shard_map/scan/all_to_all | solution.py:560
  128.1 15.5 %carried.1.refs_7_.refs_0_ = bf16[256,256]{1,0:T(8,128)(2,1)} custom-call(bf16[256,128]{1,0:T(8,128)(2,1)} %refs_0_.1, f32[1,128]{1,0:T(1,128)} %bitcast.18, f32[1,128]{1,0:T(1,128)} %bitcast.20, f32[256,128]{1,0:T(8,128)} %get-tuple-element.21.step_ref.refs_3_.refs_0_, f32[256,128]{1,0:T(8,128)} %get-tuple-element.22.after_ref.cum_ref.refs_4_.refs_1_, ...), custom_call_target="tpu_custom_call" | custom-call | flops 1000 | bytes 1000 | tf_op jit(solution)/shard_map/carried/pallas_call | solution.py:651
  143.6 2.2 %collective-permute-start.11 = (bf16[256,256]{1,0:T(8,128)(2,1)}, bf16[256,256]{1,0:T(8,128)(2,1)}, u32[]{:S(2)}, u32[]{:S(2)}) collective-permute-start(bf16[256,256]{1,0:T(8,128)(2,1)} %carried.1.refs_7_.refs_0_), channel_id=1, source_target_pairs={{0,6},{1,7},{2,4},{3,5},{4,2},{5,3},{6,0},{7,1},{8,14},{9,15},{10,... | collective-permute-start | bytes 393224 | tf_op jit(solution)/shard_map/projection/ppermute | solution.py:492
  145.8 0.6 collective-permute-start.9
  146.4 0.7 collective-permute-start.7
  147.1 1.0 collective-permute-start.6
  148.1 2.7 %collective-permute-done.11.refs_6_ = bf16[256,256]{1,0:T(8,128)(2,1)} collective-permute-done((bf16[256,256]{1,0:T(8,128)(2,1)}, bf16[256,256]{1,0:T(8,128)(2,1)}, u32[]{:S(2)}, u32[]{:S(2)}) %collective-permute-start.11) | collective-permute-done | bytes 131104 | tf_op jit(solution)/shard_map/projection/ppermute | solution.py:492
  150.8 0.3 collective-permute-start.12
  151.2 2.9 %collective-permute-done.9.refs_4_ = bf16[256,256]{1,0:T(8,128)(2,1)} collective-permute-done((bf16[256,256]{1,0:T(8,128)(2,1)}, bf16[256,256]{1,0:T(8,128)(2,1)}, u32[]{:S(2)}, u32[]{:S(2)}) %collective-permute-start.9) | collective-permute-done | bytes 131104 | tf_op jit(solution)/shard_map/projection/ppermute | solution.py:492
  154.0 0.1 collective-permute-start.10
  154.1 0.3 collective-permute-done.7.refs_2_
  154.4 0.2 collective-permute-start.8
  154.6 0.0 collective-permute-done.13.refs_8_.refs_15_
  154.6 3.8 %grad_x.1.refs_16_.refs_8_ = bf16[256,8192]{1,0:T(8,128)(2,1)} custom-call(f32[256,128]{1,0:T(8,128)} %get-tuple-element.21.step_ref.refs_3_.refs_0_, f32[256,128]{1,0:T(8,128)} %get-tuple-element.22.after_ref.cum_ref.refs_4_.refs_1_, bf16[64,256]{1,0:T(8,128)(2,1)} %bitcast.10, f32[1,128]{1,0:T(1,128)} %bitcast.15, bf16[256,8192]{1,0:T(8,128)(2,1)} %refs_4_.3, ...), custom_call_target="tpu_custom_call" | custom-call | flops 1000 | bytes 1000 | tf_op jit(solution)/shard_map/grad_x/pallas_call | solution.py:677
  158.4 0.0 collective-permute-done.6.refs_1_
  158.4 0.0 collective-permute-done.12.refs_7_
  158.4 0.0 collective-permute-done.10.refs_5_
  158.4 0.0 collective-permute-done.8.refs_3_
  158.4 6.1 %projection.3 = (bf16[264,256]{1,0:T(8,128)(2,1)}, bf16[264,256]{1,0:T(8,128)(2,1)}, bf16[264,256]{1,0:T(8,128)(2,1)}, bf16[264,256]{1,0:T(8,128)(2,1)}) custom-call(s32[2]{0:T(128)} %pad_add_fusion.place_ref, bf16[256,256]{1,0:T(8,128)(2,1)} %carried.1.refs_7_.refs_0_, bf16[256,256]{1,0:T(8,128)(2,1)} %collective-permute-done.6.refs_1_, ...), custom_call_target="tpu_custom_call" | custom-call | flops 1000 | bytes 1000 | tf_op jit(solution)/shard_map/projection/pallas_call | solution.py:696
  164.5 1.8 collective-permute-start.14
  166.2 0.7 collective-permute-start.15
  167.0 2.0 %collective-permute-start.16 = (bf16[264,256]{1,0:T(8,128)(2,1)}, bf16[264,256]{1,0:T(8,128)(2,1)}, u32[]{:S(2)}, u32[]{:S(2)}) collective-permute-start(bf16[264,256]{1,0:T(8,128)(2,1)} %get-tuple-element.39), channel_id=1, source_target_pairs={{0,24},{8,16},{16,8},{24,0},{1,25},{9,17},{17,9},{25,1},{2,26},{10... | collective-permute-start | bytes 405512 | tf_op jit(solution)/shard_map/projection/ppermute | solution.py:492
  169.0 7.6 %projection.4.refs_4_ = bf16[256,8192]{1,0:T(8,128)(2,1)} custom-call(f32[256,128]{1,0:T(8,128)} %get-tuple-element.21.step_ref.refs_3_.refs_0_, f32[256,128]{1,0:T(8,128)} %get-tuple-element.22.after_ref.cum_ref.refs_4_.refs_1_, bf16[64,256]{1,0:T(8,128)(2,1)} %bitcast.11, f32[1,128]{1,0:T(1,128)} %bitcast.16, ...), custom_call_target="tpu_custom_call", output_to_operand_aliasing={{}: (8, {})} | custom-call | flops 1000 | bytes 1000 | tf_op jit(solution)/shard_map/projection/pallas_call | solution.py:677
  176.5 0.0 collective-permute-done.14.refs_1_
  176.5 3.2 %collective-permute-done.15.refs_2_ = bf16[264,256]{1,0:T(8,128)(2,1)} collective-permute-done((bf16[264,256]{1,0:T(8,128)(2,1)}, bf16[264,256]{1,0:T(8,128)(2,1)}, u32[]{:S(2)}, u32[]{:S(2)}) %collective-permute-start.15) | collective-permute-done | bytes 135200 | tf_op jit(solution)/shard_map/projection/ppermute | solution.py:492
  179.7 0.0 collective-permute-done.16.refs_3_
  179.7 2.2 %projection.5 = f32[256,256]{1,0:T(8,128)} custom-call(bf16[264,256]{1,0:T(8,128)(2,1)} %get-tuple-element.36.refs_7_.refs_0_, bf16[264,256]{1,0:T(8,128)(2,1)} %collective-permute-done.14.refs_1_, bf16[264,256]{1,0:T(8,128)(2,1)} %collective-permute-done.15.refs_2_, bf16[264,256]{1,0:T(8,128)(2,1)} %collective-permute-done.16.refs_3_, ...), custom_call_target="tpu_custom_call" | custom-call | flops 1000 | bytes 1000 | tf_op jit(solution)/shard_map/projection/pallas_call | solution.py:711
  (2 shorter events, 0.0 us)
Async XLA Ops:
  10.4 57.9 %all-to-all-start = ((bf16[32,136,256]{2,1,0:T(8,128)(2,1)}), bf16[32,136,256]{2,1,0:T(8,128)(2,1)}, u32[]{:S(2)}, u32[]{:S(2)}) async-start(bf16[32,136,256]{2,1,0:T(8,128)(2,1)} %get-tuple-element.25), calls=%async_computation | async-start | bytes 4456448 | tf_op jit(solution)/shard_map/scan/all_to_all | solution.py:560
  24.0 33.5 %collective-permute-start = (bf16[4,256,256]{2,1,0:T(8,128)(2,1)}, bf16[4,256,256]{2,1,0:T(8,128)(2,1)}, u32[]{:S(2)}, u32[]{:S(2)}) collective-permute-start(bf16[4,256,256]{2,1,0:T(8,128)(2,1)} %get-tuple-element.27), channel_id=1, source_target_pairs={{0,1},{1,0},{2,3},{3,2},{4,5},{5,4},{6,7},{7,6},{8,9},{9,8},{10,11... | collective-permute-start | bytes 1572872 | tf_op jit(solution)/shard_map/layer/ppermute | solution.py:492
  24.3 33.2 %collective-permute-start.1 = (bf16[4,256,256]{2,1,0:T(8,128)(2,1)}, bf16[4,256,256]{2,1,0:T(8,128)(2,1)}, u32[]{:S(2)}, u32[]{:S(2)}) collective-permute-start(bf16[4,256,256]{2,1,0:T(8,128)(2,1)} %get-tuple-element.28), channel_id=1, source_target_pairs={{0,2},{1,3},{2,0},{3,1},{4,6},{5,7},{6,4},{7,5},{8,10},{9,11},{10,... | collective-permute-start | bytes 1572872 | tf_op jit(solution)/shard_map/layer/ppermute | solution.py:492
  26.0 31.6 %collective-permute-start.2 = (bf16[4,256,256]{2,1,0:T(8,128)(2,1)}, bf16[4,256,256]{2,1,0:T(8,128)(2,1)}, u32[]{:S(2)}, u32[]{:S(2)}) collective-permute-start(bf16[4,256,256]{2,1,0:T(8,128)(2,1)} %get-tuple-element.29), channel_id=1, source_target_pairs={{0,4},{1,5},{2,6},{3,7},{4,0},{5,1},{6,2},{7,3},{8,12},{9,13},{10,... | collective-permute-start | bytes 1572872 | tf_op jit(solution)/shard_map/layer/ppermute | solution.py:492
  27.4 38.5 %collective-permute-start.3 = (bf16[4,256,256]{2,1,0:T(8,128)(2,1)}, bf16[4,256,256]{2,1,0:T(8,128)(2,1)}, u32[]{:S(2)}, u32[]{:S(2)}) collective-permute-start(bf16[4,256,256]{2,1,0:T(8,128)(2,1)} %get-tuple-element.30), channel_id=1, source_target_pairs={{0,3},{1,2},{2,1},{3,0},{4,7},{5,6},{6,5},{7,4},{8,11},{9,10},{10,... | collective-permute-start | bytes 1572872 | tf_op jit(solution)/shard_map/layer/ppermute | solution.py:492
  27.4 39.1 %collective-permute-start.4 = (bf16[4,256,256]{2,1,0:T(8,128)(2,1)}, bf16[4,256,256]{2,1,0:T(8,128)(2,1)}, u32[]{:S(2)}, u32[]{:S(2)}) collective-permute-start(bf16[4,256,256]{2,1,0:T(8,128)(2,1)} %get-tuple-element.31), channel_id=1, source_target_pairs={{0,5},{1,4},{2,7},{3,6},{4,1},{5,0},{6,3},{7,2},{8,13},{9,12},{10,... | collective-permute-start | bytes 1572872 | tf_op jit(solution)/shard_map/layer/ppermute | solution.py:492
  73.7 4.5 %copy-start = (bf16[4,256,256]{2,1,0:T(8,128)(2,1)S(1)}, bf16[4,256,256]{2,1,0:T(8,128)(2,1)}, u32[]{:S(2)}) copy-start(bf16[4,256,256]{2,1,0:T(8,128)(2,1)} %get-tuple-element.34) | copy-start | bytes 1572868
  73.7 54.4 %all-to-all-start.1 = ((bf16[32,136,256]{2,1,0:T(8,128)(2,1)}), bf16[32,136,256]{2,1,0:T(8,128)(2,1)}, u32[]{:S(2)}, u32[]{:S(2)}) async-start(bf16[32,136,256]{2,1,0:T(8,128)(2,1)} %scan.1), calls=%async_computation.1 | async-start | bytes 4456448 | tf_op jit(solution)/shard_map/scan/all_to_all | solution.py:560
  78.3 38.6 %collective-permute-start.5 = (bf16[4,256,256]{2,1,0:T(8,128)(2,1)S(1)}, bf16[4,256,256]{2,1,0:T(8,128)(2,1)}, u32[]{:S(2)}, u32[]{:S(2)}) collective-permute-start(bf16[4,256,256]{2,1,0:T(8,128)(2,1)S(1)} %copy-done), channel_id=1, source_target_pairs={{0,6},{1,7},{2,4},{3,5},{4,2},{5,3},{6,0},{7,1},{8,14},{9,15},{10,... | collective-permute-start | bytes 1572872 | tf_op jit(solution)/shard_map/layer/ppermute | solution.py:492
  80.8 73.8 %collective-permute-start.13 = (bf16[4,256,256]{2,1,0:T(8,128)(2,1)}, bf16[4,256,256]{2,1,0:T(8,128)(2,1)}, u32[]{:S(2)}, u32[]{:S(2)}) collective-permute-start(bf16[4,256,256]{2,1,0:T(8,128)(2,1)} %get-tuple-element.35), channel_id=1, source_target_pairs={{0,7},{1,6},{2,5},{3,4},{4,3},{5,2},{6,1},{7,0},{8,15},{9,14},{10,... | collective-permute-start | bytes 1572872 | tf_op jit(solution)/shard_map/layer/ppermute | solution.py:492
  143.6 7.2 %collective-permute-start.11 = (bf16[256,256]{1,0:T(8,128)(2,1)}, bf16[256,256]{1,0:T(8,128)(2,1)}, u32[]{:S(2)}, u32[]{:S(2)}) collective-permute-start(bf16[256,256]{1,0:T(8,128)(2,1)} %carried.1.refs_7_.refs_0_), channel_id=1, source_target_pairs={{0,6},{1,7},{2,4},{3,5},{4,2},{5,3},{6,0},{7,1},{8,14},{9,15},{10,... | collective-permute-start | bytes 393224 | tf_op jit(solution)/shard_map/projection/ppermute | solution.py:492
  145.8 8.2 %collective-permute-start.9 = (bf16[256,256]{1,0:T(8,128)(2,1)}, bf16[256,256]{1,0:T(8,128)(2,1)}, u32[]{:S(2)}, u32[]{:S(2)}) collective-permute-start(bf16[256,256]{1,0:T(8,128)(2,1)} %carried.1.refs_7_.refs_0_), channel_id=1, source_target_pairs={{0,4},{1,5},{2,6},{3,7},{4,0},{5,1},{6,2},{7,3},{8,12},{9,13},{10,... | collective-permute-start | bytes 393224 | tf_op jit(solution)/shard_map/projection/ppermute | solution.py:492
  146.4 8.0 %collective-permute-start.7 = (bf16[256,256]{1,0:T(8,128)(2,1)}, bf16[256,256]{1,0:T(8,128)(2,1)}, u32[]{:S(2)}, u32[]{:S(2)}) collective-permute-start(bf16[256,256]{1,0:T(8,128)(2,1)} %carried.1.refs_7_.refs_0_), channel_id=1, source_target_pairs={{0,2},{1,3},{2,0},{3,1},{4,6},{5,7},{6,4},{7,5},{8,10},{9,11},{10,... | collective-permute-start | bytes 393224 | tf_op jit(solution)/shard_map/projection/ppermute | solution.py:492
  147.1 11.2 %collective-permute-start.6 = (bf16[256,256]{1,0:T(8,128)(2,1)}, bf16[256,256]{1,0:T(8,128)(2,1)}, u32[]{:S(2)}, u32[]{:S(2)}) collective-permute-start(bf16[256,256]{1,0:T(8,128)(2,1)} %carried.1.refs_7_.refs_0_), channel_id=1, source_target_pairs={{0,1},{1,0},{2,3},{3,2},{4,5},{5,4},{6,7},{7,6},{8,9},{9,8},{10,11... | collective-permute-start | bytes 393224 | tf_op jit(solution)/shard_map/projection/ppermute | solution.py:492
  150.8 7.5 %collective-permute-start.12 = (bf16[256,256]{1,0:T(8,128)(2,1)}, bf16[256,256]{1,0:T(8,128)(2,1)}, u32[]{:S(2)}, u32[]{:S(2)}) collective-permute-start(bf16[256,256]{1,0:T(8,128)(2,1)} %collective-permute-done.11.refs_6_), channel_id=1, source_target_pairs={{0,1},{1,0},{2,3},{3,2},{4,5},{5,4},{6,7},{7,6},{8,9},{9,8},{10,11... | collective-permute-start | bytes 393224 | tf_op jit(solution)/shard_map/projection/ppermute | solution.py:492
  154.0 4.3 %collective-permute-start.10 = (bf16[256,256]{1,0:T(8,128)(2,1)}, bf16[256,256]{1,0:T(8,128)(2,1)}, u32[]{:S(2)}, u32[]{:S(2)}) collective-permute-start(bf16[256,256]{1,0:T(8,128)(2,1)} %collective-permute-done.9.refs_4_), channel_id=1, source_target_pairs={{0,1},{1,0},{2,3},{3,2},{4,5},{5,4},{6,7},{7,6},{8,9},{9,8},{10,11... | collective-permute-start | bytes 393224 | tf_op jit(solution)/shard_map/projection/ppermute | solution.py:492
  154.4 4.0 %collective-permute-start.8 = (bf16[256,256]{1,0:T(8,128)(2,1)}, bf16[256,256]{1,0:T(8,128)(2,1)}, u32[]{:S(2)}, u32[]{:S(2)}) collective-permute-start(bf16[256,256]{1,0:T(8,128)(2,1)} %collective-permute-done.7.refs_2_), channel_id=1, source_target_pairs={{0,1},{1,0},{2,3},{3,2},{4,5},{5,4},{6,7},{7,6},{8,9},{9,8},{10,11... | collective-permute-start | bytes 393224 | tf_op jit(solution)/shard_map/projection/ppermute | solution.py:492
  164.5 12.1 %collective-permute-start.14 = (bf16[264,256]{1,0:T(8,128)(2,1)}, bf16[264,256]{1,0:T(8,128)(2,1)}, u32[]{:S(2)}, u32[]{:S(2)}) collective-permute-start(bf16[264,256]{1,0:T(8,128)(2,1)} %get-tuple-element.37), channel_id=1, source_target_pairs={{0,8},{8,0},{16,24},{24,16},{1,9},{9,1},{17,25},{25,17},{2,10},{10... | collective-permute-start | bytes 405512 | tf_op jit(solution)/shard_map/projection/ppermute | solution.py:492
  166.2 13.5 %collective-permute-start.15 = (bf16[264,256]{1,0:T(8,128)(2,1)}, bf16[264,256]{1,0:T(8,128)(2,1)}, u32[]{:S(2)}, u32[]{:S(2)}) collective-permute-start(bf16[264,256]{1,0:T(8,128)(2,1)} %get-tuple-element.38), channel_id=1, source_target_pairs={{0,16},{8,24},{16,0},{24,8},{1,17},{9,25},{17,1},{25,9},{2,18},{10... | collective-permute-start | bytes 405512 | tf_op jit(solution)/shard_map/projection/ppermute | solution.py:492
  167.0 12.8 %collective-permute-start.16 = (bf16[264,256]{1,0:T(8,128)(2,1)}, bf16[264,256]{1,0:T(8,128)(2,1)}, u32[]{:S(2)}, u32[]{:S(2)}) collective-permute-start(bf16[264,256]{1,0:T(8,128)(2,1)} %get-tuple-element.39), channel_id=1, source_target_pairs={{0,24},{8,16},{16,8},{24,0},{1,25},{9,17},{17,9},{25,1},{2,26},{10... | collective-permute-start | bytes 405512 | tf_op jit(solution)/shard_map/projection/ppermute | solution.py:492

commit v2 on v1

--- a/solution.py
+++ b/solution.py
@@ -408,29 +408,34 @@
         table_ref[...] = jnp.concatenate([raw_grad.T, map_grad.T], axis=0).astype(BF16)
 
 
-def grad_kernel(head_width, scale, first_head, waits, *refs):
-    step_ref, cum_ref, write_ref, skip_ref, dy_ref, inner_ref, answer_ref = refs[:7]
-    grad_ref, weight_e, maps, picks = refs[7 + waits :]
+def grad_setup_kernel(scale, step_ref, cum_ref, write_ref, *rest):
+    weight_ref, maps_ref = rest[-2:]
+    cum = cum_ref[...]
+    finish = cum[cum.shape[0] - 1 :, :]
+    weight_ref[...] = step_ref[...] * jnp.exp(finish - cum) * scale
+    write = write_ref[...].astype(F32).T.astype(BF16)
+    maps_ref[...] = jnp.concatenate([write, write], axis=1)
+
+
+def grad_kernel(head_width, *refs):
+    weight_ref, maps_ref, skip_ref, dy_ref, inner_ref, answer_ref = refs[:6]
+    grad_ref, picks = refs[-2:]
     turn = pl.program_id(0)
-    rows, lanes = dy_ref.shape
-    heads = step_ref.shape[1]
-    state = write_ref.shape[0]
+    lanes = dy_ref.shape[1]
+    heads = skip_ref.shape[1]
+    state = maps_ref.shape[1] // 2
     group = lanes // head_width
 
     @pl.when(turn == 0)
     def _():
-        cum = cum_ref[...]
-        finish = cum[rows - 1 : rows, :]
-        weight_e[...] = step_ref[...] * jnp.exp(finish - cum) * scale
-        write = write_ref[...].astype(F32).T.astype(BF16)
-        maps[...] = jnp.concatenate([write, write], axis=1)
         picks[...] = spread_picks(group, heads, lanes, head_width)
 
-    first_here = first_head + turn * group
+    first_here = turn * group
     end_parts = jnp.concatenate(halves(read_answer(answer_ref, state, 1)), axis=0)
     skip = jnp.broadcast_to(skip_ref[...], (16, heads))
     skip = spread_heads(skip, first_here, picks[...], group)[0:1]
-    carried = mul(maps[...], end_parts) * spread_heads(weight_e[...], first_here, picks[...], group)
+    spread = spread_heads(weight_ref[...], first_here, picks[...], group)
+    carried = mul(maps_ref[...], end_parts) * spread
     inner = inner_ref[...].astype(F32)
     grad_ref[...] = (inner + skip * dy_ref[...].astype(F32) + carried).astype(BF16)
 
@@ -669,24 +674,15 @@
             *(head_inputs, output_grad, returned, *lasts),
         )
 
-    def grad_part_of(first, last, grad, keep):
-        in_specs = [head_spec, head_spec, map_spec, line_spec]
-        in_specs += [tokens(grad_lanes, first), tokens(grad_lanes, first)]
-        in_specs += [messages(grad_lanes, first)]
-        in_specs += [anywhere] * len(grad)
-        (grad,) = call(
-            functools.partial(grad_kernel, head_width, scale, first * GRAD_HEADS, len(grad)),
-            last - first,
-            in_specs,
-            [(tokens(grad_lanes, first), (rows, channels), BF16)],
-            [((rows, heads), F32), ((rows, 2 * state), BF16), ((heads, grad_lanes), BF16)],
-            {len(in_specs) - 1: 0} if keep else {},
-        )(step, cum, write_t, skip, output_grad, inner, returned, *grad)
-        return grad
-
-    grad_steps = channels // grad_lanes
     with jax.named_scope("grad_x"):
-        grad_first = grad_part_of(0, 1, [table] + latest, False)
+        grad_maps = whole((rows, 2 * state))
+        grad_weight, grad_map = call(
+            functools.partial(grad_setup_kernel, scale),
+            1,
+            [head_spec, head_spec, map_spec] + [anywhere] * (1 + len(latest)),
+            [head_out, (grad_maps, (rows, 2 * state), BF16)],
+            [],
+        )(step, cum, write_t, table, *latest)
 
     with jax.named_scope("projection"):
         tables = [table]
@@ -705,8 +701,15 @@
             ],
             compiler_params=pltpu.CompilerParams(vmem_limit_bytes=VMEM_LIMIT),
             cost_estimate=SHORT,
-        )(place, *tables, *layer_parts, grad_first)
-        grad_x = grad_part_of(1, grad_steps, [products[0], grad_first], True)
+        )(place, *tables, *layer_parts, grad_weight)
+        (grad_x,) = call(
+            functools.partial(grad_kernel, head_width),
+            channels // grad_lanes,
+            [head_spec, grad_maps, line_spec, tokens(grad_lanes), tokens(grad_lanes)]
+            + [messages(grad_lanes), anywhere],
+            [(tokens(grad_lanes), (rows, channels), BF16)],
+            [((heads, grad_lanes), BF16)],
+        )(grad_weight, grad_map, skip, output_grad, inner, returned, products[0])
         sums = [swap(one, "seq", turn) for turn, one in enumerate(products)]
         (weight_grad,) = call(
             functools.partial(gather_kernel, 1.0 / math.sqrt(rows * blocks), planes),

time: 183 us -> 180 us (0.984)
  no operation moved by 1% of the time
where the time goes in v2:
time: 180 us
  Pallas kernels  84.6 us (47%)
  waiting for transfers between devices  65.9 us (37%)
  starting transfers between devices  28 us (16%)
    ppermute x17, waiting for transfers between devices, swap(): lax.ppermute(array, axis, [(one, one ^ turn) for one in range(count)])  53.1 us
    pallas_call x1, Pallas kernels, body(): call(functools.partial(block_kernel, head_width, scale, 0, 1), channels /...  29.5 us
    ppermute x17, starting transfers between devices, swap(): lax.ppermute(array, axis, [(one, one ^ turn) for one in range(count)])  16.1 us
    pallas_call x1, Pallas kernels, body(): call(functools.partial(carry_kernel, head_width, scale, len(lasts)), chan...  15.5 us
    all_to_all x2, waiting for transfers between devices, exchange(): return lax.all_to_all(array, axes, split_axis=0, concat_axis=0, tiled=True)  12.8 us
    all_to_all x2, starting transfers between devices, exchange(): return lax.all_to_all(array, axes, split_axis=0, concat_axis=0, tiled=True)  11.9 us
    pallas_call x1, Pallas kernels, body(): call(functools.partial(summary_kernel, head_width), channels // summary_l...  9.77 us
    pallas_call x1, Pallas kernels, body(): call(functools.partial(grad_kernel, head_width), channels // grad_lanes,...  8.61 us
  transfers between devices with their start and end apart: 19, of which 9 were waited for; matrix products, arithmetic and copies ran while one was open for 0% of the time, Pallas kernels for 34%

profile of v2, /device:TPU:0, one launch (start us, length us, event | category | flops | bytes accessed | tf_op | source)
XLA Modules:
  0.0 179.9 jit_solution(13754997597775007502)
XLA Ops:
  0.6 9.8 %summaries.1 = (bf16[32,136,256]{2,1,0:T(8,128)(2,1)}, f32[256,128]{1,0:T(8,128)}, f32[256,128]{1,0:T(8,128)}) custom-call(bf16[256,128]{1,0:T(8,128)(2,1)} %refs_0_.1, f32[1,128]{1,0:T(1,128)} %bitcast.14, f32[1,128]{1,0:T(1,128)} %bitcast.16, bf16[64,256]{1,0:T(8,128)(2,1)} %bitcast.7, bf16[64,256]{1,0:T(8,128)(2,1)} %bitcast.11, ...), custom_call_target="tpu_custom_call" | custom-call | flops 1000 | bytes 1000 | tf_op jit(solution)/shard_map/summaries/pallas_call | solution.py:581
  10.4 7.4 %all-to-all-start = ((bf16[32,136,256]{2,1,0:T(8,128)(2,1)}), bf16[32,136,256]{2,1,0:T(8,128)(2,1)}, u32[]{:S(2)}, u32[]{:S(2)}) async-start(bf16[32,136,256]{2,1,0:T(8,128)(2,1)} %get-tuple-element.29), calls=%async_computation | async-start | bytes 4456448 | tf_op jit(solution)/shard_map/scan/all_to_all | solution.py:565
  17.8 0.6 pad_add_fusion.place_ref
  18.5 5.7 %layer.1 = (bf16[4,256,256]{2,1,0:T(8,128)(2,1)}, bf16[4,256,256]{2,1,0:T(8,128)(2,1)}, bf16[4,256,256]{2,1,0:T(8,128)(2,1)}, bf16[4,256,256]{2,1,0:T(8,128)(2,1...) custom-call(s32[2]{0:T(128)} %pad_add_fusion.place_ref, ...), custom_call_target="tpu_custom_call" | custom-call | flops 1000 | bytes 1000 | tf_op jit(solution)/shard_map/layer/pallas_call | solution.py:601
  24.2 0.3 collective-permute-start
  24.4 1.7 collective-permute-start.1
  26.1 1.5 collective-permute-start.2
  27.5 0.0 collective-permute-start.3
  27.6 0.6 collective-permute-start.4
  28.2 29.5 %own_block.1 = (bf16[256,8192]{1,0:T(8,128)(2,1)}, f32[256,128]{1,0:T(8,128)}, f32[256,128]{1,0:T(8,128)}, f32[256,128]{1,0:T(8,128)}) custom-call(f32[256,128]{1,0:T(8,128)} %get-tuple-element.23.step_ref.refs_3_, f32[256,128]{1,0:T(8,128)} %get-tuple-element.24.after_ref.cum_ref.refs_4_, bf16[64,256]{1,0:T(8,128)(2,1)} %bitcast.8, ...), custom_call_target="tpu_custom_call" | custom-call | flops 1000 | bytes 1000 | tf_op jit(solution)/shard_map/own_block/pallas_call | solution.py:624
  57.7 0.0 collective-permute-done.rest_1_.refs_9_
  57.7 0.0 collective-permute-done.1.rest_2_.refs_10_
  57.7 0.0 collective-permute-done.2.rest_3_.refs_12_
  57.7 8.2 %collective-permute-done.3.rest_4_.refs_11_ = bf16[4,256,256]{2,1,0:T(8,128)(2,1)} collective-permute-done((bf16[4,256,256]{2,1,0:T(8,128)(2,1)}, bf16[4,256,256]{2,1,0:T(8,128)(2,1)}, u32[]{:S(2)}, u32[]{:S(2)}) %collective-permute-start.3) | collective-permute-done | bytes 524320 | tf_op jit(solution)/shard_map/layer/ppermute | solution.py:497
  65.9 0.8 collective-permute-done.4.rest_5_.refs_13_
  66.7 1.6 all-to-all-done.message_ref
  68.3 5.4 %scan.1 = bf16[32,136,256]{2,1,0:T(8,128)(2,1)} custom-call(bf16[32,136,256]{2,1,0:T(8,128)(2,1)} %all-to-all-done.message_ref, f32[256,128]{1,0:T(8,128)} %get-tuple-element.26.rest_0_.refs_7_, bf16[4,256,256]{2,1,0:T(8,128)(2,1)} %collective-permute-done.rest_1_.refs_9_, bf16[4,256,256]{2,1,0:T(8,128)(2,1)} %collective-permute-done.1.rest_2_.refs_10_, ...), custom_call_target="tpu_custom_call" | custom-call | flops 1000 | bytes 1000 | tf_op jit(solution)/shard_map/scan/pallas_call | solution.py:646
  73.7 4.5 %all-to-all-start.1 = ((bf16[32,136,256]{2,1,0:T(8,128)(2,1)}), bf16[32,136,256]{2,1,0:T(8,128)(2,1)}, u32[]{:S(2)}, u32[]{:S(2)}) async-start(bf16[32,136,256]{2,1,0:T(8,128)(2,1)} %scan.1), calls=%async_computation.1 | async-start | bytes 4456448 | tf_op jit(solution)/shard_map/scan/all_to_all | solution.py:565
  78.3 2.5 %collective-permute-start.5 = (bf16[4,256,256]{2,1,0:T(8,128)(2,1)S(1)}, bf16[4,256,256]{2,1,0:T(8,128)(2,1)}, u32[]{:S(2)}, u32[]{:S(2)}) collective-permute-start(bf16[4,256,256]{2,1,0:T(8,128)(2,1)S(1)} %copy-done), channel_id=1, source_target_pairs={{0,6},{1,7},{2,4},{3,5},{4,2},{5,3},{6,0},{7,1},{8,14},{9,15},{10,... | collective-permute-start | bytes 1572872 | tf_op jit(solution)/shard_map/layer/ppermute | solution.py:497
  80.8 0.0 collective-permute-start.6
  80.8 36.1 %collective-permute-done.5.refs_13_.refs_14_ = bf16[4,256,256]{2,1,0:T(8,128)(2,1)} collective-permute-done((bf16[4,256,256]{2,1,0:T(8,128)(2,1)S(1)}, bf16[4,256,256]{2,1,0:T(8,128)(2,1)}, u32[]{:S(2)}, u32[]{:S(2)}) %collective-permute-start.5) | collective-permute-done | bytes 524320 | tf_op jit(solution)/shard_map/layer/ppermute | solution.py:497
  116.9 11.3 %all-to-all-done.1.refs_12_.refs_5_ = bf16[32,136,256]{2,1,0:T(8,128)(2,1)} async-done(((bf16[32,136,256]{2,1,0:T(8,128)(2,1)}), bf16[32,136,256]{2,1,0:T(8,128)(2,1)}, u32[]{:S(2)}, u32[]{:S(2)}) %all-to-all-start.1) | async-done | bytes 2228256 | tf_op jit(solution)/shard_map/scan/all_to_all | solution.py:565
  128.1 15.5 %carried.1.rest_0_.refs_0_ = bf16[256,256]{1,0:T(8,128)(2,1)} custom-call(bf16[256,128]{1,0:T(8,128)(2,1)} %refs_0_.1, f32[1,128]{1,0:T(1,128)} %bitcast.15, f32[1,128]{1,0:T(1,128)} %bitcast.17, f32[256,128]{1,0:T(8,128)} %get-tuple-element.23.step_ref.refs_3_, f32[256,128]{1,0:T(8,128)} %get-tuple-element.24.after_ref.cum_ref.refs_4_, ...), custom_call_target="tpu_custom_call" | custom-call | flops 1000 | bytes 1000 | tf_op jit(solution)/shard_map/carried/pallas_call | solution.py:656
  143.7 2.2 %collective-permute-start.12 = (bf16[256,256]{1,0:T(8,128)(2,1)}, bf16[256,256]{1,0:T(8,128)(2,1)}, u32[]{:S(2)}, u32[]{:S(2)}) collective-permute-start(bf16[256,256]{1,0:T(8,128)(2,1)} %carried.1.rest_0_.refs_0_), channel_id=1, source_target_pairs={{0,6},{1,7},{2,4},{3,5},{4,2},{5,3},{6,0},{7,1},{8,14},{9,15},{10,... | collective-permute-start | bytes 393224 | tf_op jit(solution)/shard_map/projection/ppermute | solution.py:497
  145.8 0.6 collective-permute-start.10
  146.4 0.7 collective-permute-start.8
  147.1 1.0 collective-permute-start.7
  148.2 2.7 %collective-permute-done.12.refs_6_ = bf16[256,256]{1,0:T(8,128)(2,1)} collective-permute-done((bf16[256,256]{1,0:T(8,128)(2,1)}, bf16[256,256]{1,0:T(8,128)(2,1)}, u32[]{:S(2)}, u32[]{:S(2)}) %collective-permute-start.12) | collective-permute-done | bytes 131104 | tf_op jit(solution)/shard_map/projection/ppermute | solution.py:497
  150.9 0.3 collective-permute-start.13
  151.2 2.9 %collective-permute-done.10.refs_4_ = bf16[256,256]{1,0:T(8,128)(2,1)} collective-permute-done((bf16[256,256]{1,0:T(8,128)(2,1)}, bf16[256,256]{1,0:T(8,128)(2,1)}, u32[]{:S(2)}, u32[]{:S(2)}) %collective-permute-start.10) | collective-permute-done | bytes 131104 | tf_op jit(solution)/shard_map/projection/ppermute | solution.py:497
  154.0 0.1 collective-permute-start.11
  154.2 0.3 collective-permute-done.8.refs_2_
  154.4 0.1 collective-permute-start.9
  154.6 0.0 collective-permute-done.6.rest_1_.refs_15_
  154.6 1.8 grad_x.1
  156.3 0.0 collective-permute-done.7.refs_1_
  156.3 0.0 collective-permute-done.13.refs_7_
  156.3 0.0 collective-permute-done.11.refs_5_
  156.3 0.0 collective-permute-done.9.refs_3_
  156.4 6.1 %projection.3 = (bf16[264,256]{1,0:T(8,128)(2,1)}, bf16[264,256]{1,0:T(8,128)(2,1)}, bf16[264,256]{1,0:T(8,128)(2,1)}, bf16[264,256]{1,0:T(8,128)(2,1)}) custom-call(s32[2]{0:T(128)} %pad_add_fusion.place_ref, bf16[256,256]{1,0:T(8,128)(2,1)} %carried.1.rest_0_.refs_0_, bf16[256,256]{1,0:T(8,128)(2,1)} %collective-permute-done.7.refs_1_, ...), custom_call_target="tpu_custom_call" | custom-call | flops 1000 | bytes 1000 | tf_op jit(solution)/shard_map/projection/pallas_call | solution.py:692
  162.5 1.7 collective-permute-start.14
  164.2 0.8 collective-permute-start.15
  165.0 1.9 %collective-permute-start.16 = (bf16[264,256]{1,0:T(8,128)(2,1)}, bf16[264,256]{1,0:T(8,128)(2,1)}, u32[]{:S(2)}, u32[]{:S(2)}) collective-permute-start(bf16[264,256]{1,0:T(8,128)(2,1)} %get-tuple-element.43), channel_id=1, source_target_pairs={{0,24},{8,16},{16,8},{24,0},{1,25},{9,17},{17,9},{25,1},{2,26},{10... | collective-permute-start | bytes 405512 | tf_op jit(solution)/shard_map/projection/ppermute | solution.py:497
  166.9 8.6 %projection.4.refs_4_ = bf16[256,8192]{1,0:T(8,128)(2,1)} custom-call(f32[256,128]{1,0:T(8,128)} %get-tuple-element.37.refs_16_.refs_0_, bf16[256,128]{1,0:T(8,128)(2,1)} %get-tuple-element.38.refs_1_, f32[1,128]{1,0:T(1,128)} %bitcast.18, bf16[256,8192]{1,0:T(8,128)(2,1)} %refs_3_.1, bf16[256,8192]{1,0:T(8,128)(2,1)} %get-tuple-element.39.refs_4_, ...), custom_call_target="tpu_custom_call" | custom-call | flops 1000 | bytes 1000 | tf_op jit(solution)/shard_map/projection/pallas_call | solution.py:705
  175.5 0.0 collective-permute-done.14.refs_1_
  175.5 2.1 %collective-permute-done.15.refs_2_ = bf16[264,256]{1,0:T(8,128)(2,1)} collective-permute-done((bf16[264,256]{1,0:T(8,128)(2,1)}, bf16[264,256]{1,0:T(8,128)(2,1)}, u32[]{:S(2)}, u32[]{:S(2)}) %collective-permute-start.15) | collective-permute-done | bytes 135200 | tf_op jit(solution)/shard_map/projection/ppermute | solution.py:497
  177.7 0.0 collective-permute-done.16.refs_3_
  177.7 2.2 %projection.5 = f32[256,256]{1,0:T(8,128)} custom-call(bf16[264,256]{1,0:T(8,128)(2,1)} %get-tuple-element.40.refs_6_.refs_0_, bf16[264,256]{1,0:T(8,128)(2,1)} %collective-permute-done.14.refs_1_, bf16[264,256]{1,0:T(8,128)(2,1)} %collective-permute-done.15.refs_2_, bf16[264,256]{1,0:T(8,128)(2,1)} %collective-permute-done.16.refs_3_, ...), custom_call_target="tpu_custom_call" | custom-call | flops 1000 | bytes 1000 | tf_op jit(solution)/shard_map/projection/pallas_call | solution.py:714
  (2 shorter events, 0.0 us)
Async XLA Ops:
  10.4 57.9 %all-to-all-start = ((bf16[32,136,256]{2,1,0:T(8,128)(2,1)}), bf16[32,136,256]{2,1,0:T(8,128)(2,1)}, u32[]{:S(2)}, u32[]{:S(2)}) async-start(bf16[32,136,256]{2,1,0:T(8,128)(2,1)} %get-tuple-element.29), calls=%async_computation | async-start | bytes 4456448 | tf_op jit(solution)/shard_map/scan/all_to_all | solution.py:565
  24.2 33.5 %collective-permute-start = (bf16[4,256,256]{2,1,0:T(8,128)(2,1)}, bf16[4,256,256]{2,1,0:T(8,128)(2,1)}, u32[]{:S(2)}, u32[]{:S(2)}) collective-permute-start(bf16[4,256,256]{2,1,0:T(8,128)(2,1)} %get-tuple-element.30), channel_id=1, source_target_pairs={{0,1},{1,0},{2,3},{3,2},{4,5},{5,4},{6,7},{7,6},{8,9},{9,8},{10,11... | collective-permute-start | bytes 1572872 | tf_op jit(solution)/shard_map/layer/ppermute | solution.py:497
  24.4 33.3 %collective-permute-start.1 = (bf16[4,256,256]{2,1,0:T(8,128)(2,1)}, bf16[4,256,256]{2,1,0:T(8,128)(2,1)}, u32[]{:S(2)}, u32[]{:S(2)}) collective-permute-start(bf16[4,256,256]{2,1,0:T(8,128)(2,1)} %get-tuple-element.31), channel_id=1, source_target_pairs={{0,2},{1,3},{2,0},{3,1},{4,6},{5,7},{6,4},{7,5},{8,10},{9,11},{10,... | collective-permute-start | bytes 1572872 | tf_op jit(solution)/shard_map/layer/ppermute | solution.py:497
  26.1 31.6 %collective-permute-start.2 = (bf16[4,256,256]{2,1,0:T(8,128)(2,1)}, bf16[4,256,256]{2,1,0:T(8,128)(2,1)}, u32[]{:S(2)}, u32[]{:S(2)}) collective-permute-start(bf16[4,256,256]{2,1,0:T(8,128)(2,1)} %get-tuple-element.32), channel_id=1, source_target_pairs={{0,4},{1,5},{2,6},{3,7},{4,0},{5,1},{6,2},{7,3},{8,12},{9,13},{10,... | collective-permute-start | bytes 1572872 | tf_op jit(solution)/shard_map/layer/ppermute | solution.py:497
  27.5 38.4 %collective-permute-start.3 = (bf16[4,256,256]{2,1,0:T(8,128)(2,1)}, bf16[4,256,256]{2,1,0:T(8,128)(2,1)}, u32[]{:S(2)}, u32[]{:S(2)}) collective-permute-start(bf16[4,256,256]{2,1,0:T(8,128)(2,1)} %get-tuple-element.33), channel_id=1, source_target_pairs={{0,3},{1,2},{2,1},{3,0},{4,7},{5,6},{6,5},{7,4},{8,11},{9,10},{10,... | collective-permute-start | bytes 1572872 | tf_op jit(solution)/shard_map/layer/ppermute | solution.py:497
  27.6 39.1 %collective-permute-start.4 = (bf16[4,256,256]{2,1,0:T(8,128)(2,1)}, bf16[4,256,256]{2,1,0:T(8,128)(2,1)}, u32[]{:S(2)}, u32[]{:S(2)}) collective-permute-start(bf16[4,256,256]{2,1,0:T(8,128)(2,1)} %get-tuple-element.34), channel_id=1, source_target_pairs={{0,5},{1,4},{2,7},{3,6},{4,1},{5,0},{6,3},{7,2},{8,13},{9,12},{10,... | collective-permute-start | bytes 1572872 | tf_op jit(solution)/shard_map/layer/ppermute | solution.py:497
  73.7 4.5 %copy-start = (bf16[4,256,256]{2,1,0:T(8,128)(2,1)S(1)}, bf16[4,256,256]{2,1,0:T(8,128)(2,1)}, u32[]{:S(2)}) copy-start(bf16[4,256,256]{2,1,0:T(8,128)(2,1)} %get-tuple-element.35) | copy-start | bytes 1572868
  73.7 54.4 %all-to-all-start.1 = ((bf16[32,136,256]{2,1,0:T(8,128)(2,1)}), bf16[32,136,256]{2,1,0:T(8,128)(2,1)}, u32[]{:S(2)}, u32[]{:S(2)}) async-start(bf16[32,136,256]{2,1,0:T(8,128)(2,1)} %scan.1), calls=%async_computation.1 | async-start | bytes 4456448 | tf_op jit(solution)/shard_map/scan/all_to_all | solution.py:565
  78.3 38.6 %collective-permute-start.5 = (bf16[4,256,256]{2,1,0:T(8,128)(2,1)S(1)}, bf16[4,256,256]{2,1,0:T(8,128)(2,1)}, u32[]{:S(2)}, u32[]{:S(2)}) collective-permute-start(bf16[4,256,256]{2,1,0:T(8,128)(2,1)S(1)} %copy-done), channel_id=1, source_target_pairs={{0,6},{1,7},{2,4},{3,5},{4,2},{5,3},{6,0},{7,1},{8,14},{9,15},{10,... | collective-permute-start | bytes 1572872 | tf_op jit(solution)/shard_map/layer/ppermute | solution.py:497
  80.8 73.8 %collective-permute-start.6 = (bf16[4,256,256]{2,1,0:T(8,128)(2,1)}, bf16[4,256,256]{2,1,0:T(8,128)(2,1)}, u32[]{:S(2)}, u32[]{:S(2)}) collective-permute-start(bf16[4,256,256]{2,1,0:T(8,128)(2,1)} %get-tuple-element.36), channel_id=1, source_target_pairs={{0,7},{1,6},{2,5},{3,4},{4,3},{5,2},{6,1},{7,0},{8,15},{9,14},{10,... | collective-permute-start | bytes 1572872 | tf_op jit(solution)/shard_map/layer/ppermute | solution.py:497
  143.7 7.2 %collective-permute-start.12 = (bf16[256,256]{1,0:T(8,128)(2,1)}, bf16[256,256]{1,0:T(8,128)(2,1)}, u32[]{:S(2)}, u32[]{:S(2)}) collective-permute-start(bf16[256,256]{1,0:T(8,128)(2,1)} %carried.1.rest_0_.refs_0_), channel_id=1, source_target_pairs={{0,6},{1,7},{2,4},{3,5},{4,2},{5,3},{6,0},{7,1},{8,14},{9,15},{10,... | collective-permute-start | bytes 393224 | tf_op jit(solution)/shard_map/projection/ppermute | solution.py:497
  145.8 8.2 %collective-permute-start.10 = (bf16[256,256]{1,0:T(8,128)(2,1)}, bf16[256,256]{1,0:T(8,128)(2,1)}, u32[]{:S(2)}, u32[]{:S(2)}) collective-permute-start(bf16[256,256]{1,0:T(8,128)(2,1)} %carried.1.rest_0_.refs_0_), channel_id=1, source_target_pairs={{0,4},{1,5},{2,6},{3,7},{4,0},{5,1},{6,2},{7,3},{8,12},{9,13},{10,... | collective-permute-start | bytes 393224 | tf_op jit(solution)/shard_map/projection/ppermute | solution.py:497
  146.4 8.0 %collective-permute-start.8 = (bf16[256,256]{1,0:T(8,128)(2,1)}, bf16[256,256]{1,0:T(8,128)(2,1)}, u32[]{:S(2)}, u32[]{:S(2)}) collective-permute-start(bf16[256,256]{1,0:T(8,128)(2,1)} %carried.1.rest_0_.refs_0_), channel_id=1, source_target_pairs={{0,2},{1,3},{2,0},{3,1},{4,6},{5,7},{6,4},{7,5},{8,10},{9,11},{10,... | collective-permute-start | bytes 393224 | tf_op jit(solution)/shard_map/projection/ppermute | solution.py:497
  147.1 9.2 %collective-permute-start.7 = (bf16[256,256]{1,0:T(8,128)(2,1)}, bf16[256,256]{1,0:T(8,128)(2,1)}, u32[]{:S(2)}, u32[]{:S(2)}) collective-permute-start(bf16[256,256]{1,0:T(8,128)(2,1)} %carried.1.rest_0_.refs_0_), channel_id=1, source_target_pairs={{0,1},{1,0},{2,3},{3,2},{4,5},{5,4},{6,7},{7,6},{8,9},{9,8},{10,11... | collective-permute-start | bytes 393224 | tf_op jit(solution)/shard_map/projection/ppermute | solution.py:497
  150.9 5.5 %collective-permute-start.13 = (bf16[256,256]{1,0:T(8,128)(2,1)}, bf16[256,256]{1,0:T(8,128)(2,1)}, u32[]{:S(2)}, u32[]{:S(2)}) collective-permute-start(bf16[256,256]{1,0:T(8,128)(2,1)} %collective-permute-done.12.refs_6_), channel_id=1, source_target_pairs={{0,1},{1,0},{2,3},{3,2},{4,5},{5,4},{6,7},{7,6},{8,9},{9,8},{10,11... | collective-permute-start | bytes 393224 | tf_op jit(solution)/shard_map/projection/ppermute | solution.py:497
  154.0 2.3 %collective-permute-start.11 = (bf16[256,256]{1,0:T(8,128)(2,1)}, bf16[256,256]{1,0:T(8,128)(2,1)}, u32[]{:S(2)}, u32[]{:S(2)}) collective-permute-start(bf16[256,256]{1,0:T(8,128)(2,1)} %collective-permute-done.10.refs_4_), channel_id=1, source_target_pairs={{0,1},{1,0},{2,3},{3,2},{4,5},{5,4},{6,7},{7,6},{8,9},{9,8},{10,11... | collective-permute-start | bytes 393224 | tf_op jit(solution)/shard_map/projection/ppermute | solution.py:497
  154.4 1.9 %collective-permute-start.9 = (bf16[256,256]{1,0:T(8,128)(2,1)}, bf16[256,256]{1,0:T(8,128)(2,1)}, u32[]{:S(2)}, u32[]{:S(2)}) collective-permute-start(bf16[256,256]{1,0:T(8,128)(2,1)} %collective-permute-done.8.refs_2_), channel_id=1, source_target_pairs={{0,1},{1,0},{2,3},{3,2},{4,5},{5,4},{6,7},{7,6},{8,9},{9,8},{10,11... | collective-permute-start | bytes 393224 | tf_op jit(solution)/shard_map/projection/ppermute | solution.py:497
  162.5 13.1 %collective-permute-start.14 = (bf16[264,256]{1,0:T(8,128)(2,1)}, bf16[264,256]{1,0:T(8,128)(2,1)}, u32[]{:S(2)}, u32[]{:S(2)}) collective-permute-start(bf16[264,256]{1,0:T(8,128)(2,1)} %get-tuple-element.41), channel_id=1, source_target_pairs={{0,8},{8,0},{16,24},{24,16},{1,9},{9,1},{17,25},{25,17},{2,10},{10... | collective-permute-start | bytes 405512 | tf_op jit(solution)/shard_map/projection/ppermute | solution.py:497
  164.2 13.5 %collective-permute-start.15 = (bf16[264,256]{1,0:T(8,128)(2,1)}, bf16[264,256]{1,0:T(8,128)(2,1)}, u32[]{:S(2)}, u32[]{:S(2)}) collective-permute-start(bf16[264,256]{1,0:T(8,128)(2,1)} %get-tuple-element.42), channel_id=1, source_target_pairs={{0,16},{8,24},{16,0},{24,8},{1,17},{9,25},{17,1},{25,9},{2,18},{10... | collective-permute-start | bytes 405512 | tf_op jit(solution)/shard_map/projection/ppermute | solution.py:497
  165.0 12.7 %collective-permute-start.16 = (bf16[264,256]{1,0:T(8,128)(2,1)}, bf16[264,256]{1,0:T(8,128)(2,1)}, u32[]{:S(2)}, u32[]{:S(2)}) collective-permute-start(bf16[264,256]{1,0:T(8,128)(2,1)} %get-tuple-element.43), channel_id=1, source_target_pairs={{0,24},{8,16},{16,8},{24,0},{1,25},{9,17},{17,9},{25,1},{2,26},{10... | collective-permute-start | bytes 405512 | tf_op jit(solution)/shard_map/projection/ppermute | solution.py:497
